TPU v7x, 32 devices: a whole 2x2x4 slice. The times are simulated.
32 devices in a mesh: dp: 16 (over z, x, core), mp: 2 (over y).
Axes of the slice: x: 2, y: 2, z: 4, core: 2. Of those that a mesh axis runs over, the one named last changes fastest.
Arguments:
- tokens: bfloat16 [16384, 1152], P('dp'), may hold values from -8 to 8
- lengths: int32 [256], P('dp'), may hold values from 1 to 64, as said below
- images: bfloat16 [256, 1152], P('dp'), may hold values from -12 to 12
- pair_group: int32 [256], replicated, may hold values from 0 to 127, never falling along the last dimension, each value on 1 to 4 neighbouring positions
- w_up: bfloat16 [1152, 4304], P(None, 'mp'), may hold values from -0.1875 to 0.1875
- w_down: bfloat16 [1152, 4304], P(None, 'mp'), may hold values from -0.09375 to 0.09375
Outputs:
- caption_loss: float32 [256], P('dp')
- image_grad: float32 [256, 1152], P('dp')
- up_grad: float32 [1152, 4304], P('dp', 'mp')
- down_grad: float32 [1152, 4304], P('dp', 'mp')
Inputs may be any that keep to these rules, and one draw needn't show every extreme that they name: Positions below lengths[c] of caption c are real tokens, the rest padding. `pair_group`: ids never fall along the pairs, and each id is held by 1 to 4 consecutive pairs.
All inputs are finite; a program needn't handle non-finite values.
Results may differ from a plain program's by a relative error of at most 0.0033.
Values may be sent and summed in bfloat16 or wider, within the bound.
A program may use at most 192 MiB of HBM per device.

v0:
```python
import jax
import jax.numpy as jnp
from jax import lax
from jax.sharding import PartitionSpec as P

LOGIT_SCALE = 117.0
LOGIT_SHIFT = -12.9


def passed_along(value, axis, steps):
    count = lax.axis_size(axis)
    pairs = [(source, (source + steps) % count) for source in range(count)]
    return lax.ppermute(value, axis, pairs)


def layer_norm(rows):
    center = rows - jnp.mean(rows, -1, keepdims=True)
    spread = jnp.mean(center * center, -1, keepdims=True)
    return center * lax.rsqrt(spread + 1e-06)


def gelu_pair(pre):
    const = 0.7978845608028654
    inner = const * (pre + 0.044715 * pre * pre * pre)
    tanh_u = jnp.tanh(inner)
    value = 0.5 * pre * (1.0 + tanh_u)
    slope = 0.5 * (1.0 + tanh_u) + 0.5 * pre * (1.0 - tanh_u * tanh_u) * const * (
        1.0 + 3.0 * 0.044715 * pre * pre
    )
    return (value, slope)


def unit_rows(rows):
    scale = lax.rsqrt(jnp.sum(rows * rows, 1, keepdims=True) + 1e-06)
    return (rows * scale, scale)


def pair_terms(text_rows, text_group, image_half, image_group, total):
    logits = (
        LOGIT_SCALE
        * lax.dot_general(
            text_rows, image_half, (((1,), (1,)), ((), ())), preferred_element_type=jnp.float32
        )
        + LOGIT_SHIFT
    )
    signs = jnp.where(text_group[:, None] == image_group[None, :], 1.0, -1.0).astype(jnp.float32)
    loss_terms = -jnp.sum(jax.nn.log_sigmoid(signs * logits), 1) / total
    coef = (-LOGIT_SCALE * signs * jax.nn.sigmoid(-signs * logits)).astype(jnp.bfloat16)
    grad_terms = jnp.dot(coef, image_half, preferred_element_type=jnp.float32)
    image_terms = lax.dot_general(
        coef, text_rows, (((0,), (0,)), ((), ())), preferred_element_type=jnp.float32
    )
    return (loss_terms, grad_terms, image_terms)


def on_device(tokens, lengths, images, pair_group, w_up, w_down):
    captions = lengths.shape[0]
    seq_len = tokens.shape[0] // captions
    width = tokens.shape[1]
    hidden = w_up.shape[1]
    devices = lax.axis_size("dp")
    own_index = lax.axis_index("dp")
    total = captions * devices
    tok_float = tokens.astype(jnp.float32)
    normed = layer_norm(tok_float).astype(jnp.bfloat16)
    pre = jnp.dot(normed, w_up, preferred_element_type=jnp.float32)
    value, slope = gelu_pair(pre)
    position = jnp.arange(seq_len, dtype=jnp.int32)
    valid = (position[None, :] < lengths[:, None]).astype(jnp.float32)
    share = valid / jnp.sum(valid, 1, keepdims=True)
    gmean = jnp.sum(value.reshape(captions, seq_len, hidden) * share[:, :, None], 1)
    tmean = jnp.sum(tok_float.reshape(captions, seq_len, width) * share[:, :, None], 1)
    gbar = gmean.astype(jnp.bfloat16)
    partial_value = lax.dot_general(
        gbar, w_down, (((1,), (1,)), ((), ())), preferred_element_type=jnp.float32
    )
    pooled = tmean + lax.psum(partial_value, "mp")
    unit_text, text_scale = unit_rows(pooled)
    unit_image, image_scale = unit_rows(images.astype(jnp.float32))
    text_half = unit_text.astype(jnp.bfloat16)
    image_half = unit_image.astype(jnp.bfloat16)
    image_group = lax.dynamic_slice_in_dim(pair_group, own_index * captions, captions)

    def visit(turn, text_rows, acc_grad, acc_loss, img_back):
        anchor = (own_index - turn) % devices
        text_group = lax.dynamic_slice_in_dim(pair_group, anchor * captions, captions)
        loss_terms, grad_terms, image_terms = pair_terms(
            text_rows, text_group, image_half, image_group, total
        )
        return (acc_grad + grad_terms, acc_loss + loss_terms, img_back + image_terms)

    def carry_home(acc_grad, acc_loss):
        return passed_along((acc_grad, acc_loss), "dp", 1)

    def cycle_step(turn, state):
        text_rows, acc_grad, acc_loss, img_back = state
        acc_grad, acc_loss, img_back = visit(turn, text_rows, acc_grad, acc_loss, img_back)
        text_rows = passed_along(text_rows, "dp", 1)
        acc_grad, acc_loss = carry_home(acc_grad, acc_loss)
        return (text_rows, acc_grad, acc_loss, img_back)

    start = (
        text_half,
        jnp.zeros((captions, width), jnp.float32),
        jnp.zeros((captions,), jnp.float32),
        jnp.zeros((captions, width), jnp.float32),
    )
    text_rows, acc_grad, acc_loss, img_back = lax.fori_loop(0, devices - 1, cycle_step, start)
    acc_grad, acc_loss, img_back = visit(devices - 1, text_rows, acc_grad, acc_loss, img_back)
    text_back, caption_loss = carry_home(acc_grad, acc_loss)
    pooled_grad = (
        text_back - unit_text * jnp.sum(unit_text * text_back, 1, keepdims=True)
    ) * text_scale
    image_grad = (
        img_back - unit_image * jnp.sum(unit_image * img_back, 1, keepdims=True)
    ) * image_scale
    pooled_half = pooled_grad.astype(jnp.bfloat16)
    hidden_grad = jnp.dot(pooled_half, w_down, preferred_element_type=jnp.float32)
    pre_grad = (
        share[:, :, None] * hidden_grad[:, None, :] * slope.reshape(captions, seq_len, hidden)
    ).astype(jnp.bfloat16)
    pre_grad = pre_grad.reshape(captions * seq_len, hidden)
    down_term = lax.dot_general(
        pooled_half, gbar, (((0,), (0,)), ((), ())), preferred_element_type=jnp.float32
    )
    both = lax.psum_scatter(
        jnp.concatenate(
            [
                lax.dot_general(
                    normed, pre_grad, (((0,), (0,)), ((), ())), preferred_element_type=jnp.float32
                ),
                down_term,
            ],
            1,
        ),
        "dp",
        scatter_dimension=0,
        tiled=True,
    )
    up_grad = both[:, :hidden]
    down_grad = both[:, hidden:]
    return (caption_loss, image_grad, up_grad, down_grad)


def solution(mesh):
    in_specs = (P("dp", None), P("dp"), P("dp", None), P(), P(None, "mp"), P(None, "mp"))
    out_specs = (P("dp"), P("dp", None), P("dp", "mp"), P("dp", "mp"))
    return jax.shard_map(
        on_device, mesh=mesh, in_specs=in_specs, out_specs=out_specs, check_vma=False
    )
```

profile of v0, /device:TPU:0, one launch (start us, length us, event | category | flops | bytes accessed | tf_op | source)
XLA Modules:
  0.0 470.5 jit_solution(4077646393957839462)
XLA Ops:
  8.0 2.0 convert_reduce_fusion
  10.1 2.4 multiply_reduce_fusion.1
  13.3 14.8 %add_multiply_fusion = (f32[1024,2152]{0,1:T(8,128)}, f32[1024,2152]{0,1:T(8,128)}) fusion(bf16[1152,2152]{0,1:T(8,128)(2,1)} %param.12, bf16[1024,1152]{1,0:T(8,128)(2,1)} %param.8, f32[1024]{0:T(1024)S(1)} %add_rsqrt_fusion, f32[1024]{0:T(1024)S(1)} %broadcast_multiply_fusion), kind=kOutput, calls=%fused_computation.29 | convolution fusion | flops 5099552768 | bytes 24954880 | tf_op jit(solution)/shard_map/dot_general | solution.py:66
  28.1 9.2 %copy.17 = f32[1024,2152]{1,0:T(8,128)} copy(f32[1024,2152]{0,1:T(8,128)} %get-tuple-element.300) | data formatting | bytes 17629184 | tf_op jit(solution)/shard_map/mul | solution.py:26
  37.3 4.9 %multiply_reduce_fusion = bf16[16,2152]{1,0:T(8,128)(2,1)S(1)} fusion(f32[16,64]{1,0:T(8,128)S(1)} %convert_divide_fusion, f32[1024,2152]{1,0:T(8,128)} %copy.17), kind=kLoop, calls=%fused_computation.21 | loop fusion | flops 4372864 | bytes 8887552 | tf_op jit(solution)/shard_map/reduce_sum | solution.py:71
  42.2 3.8 fusion.54
  47.3 22.2 %all-reduce.2.cloned.1.call-done = f32[16,1152]{1,0:T(8,128)} async-done(((f32[16,1152]{1,0:T(8,128)}), f32[16,1152]{1,0:T(8,128)}) %all-reduce.2.cloned.1.call-update) | async-done | bytes 73744 | tf_op jit(solution)/shard_map/psum | solution.py:77
  69.5 1.0 multiply_reduce_fusion.4
  70.7 108.6 %while.22 = (s32[]{:T(128)}, bf16[16,1152]{1,0:T(8,128)(2,1)S(1)}, f32[16,1152]{1,0:T(8,128)S(1)}, f32[16]{0:T(128)S(1)}, f32[16,1152]{1,0:T(8,128)S(1)}, /*inde...) while((s32[]{:T(128)}, bf16[16,1152]{1,0:T(8,128)(2,1)S(1)}, ...), condition=%wide.region_10.11_spmd.clone, body=%wide.region_8.10_spmd.clone.sunk | while | flops 1833251 | bytes 962994 | solution.py:108
  71.0 1.6 collective-permute-start.2
  73.2 3.7 collective-permute-done.2
  76.9 2.5 collective-permute-done.1
  80.3 5.2 %collective-permute-done.2 = f32[16]{0:T(128)S(1)} collective-permute-done((f32[16]{0:T(128)S(1)}, f32[16]{0:T(128)S(1)}, u32[]{:S(2)}, u32[]{:S(2)}) %collective-permute-start.2) | collective-permute-done | bytes 96 | tf_op jit(solution)/shard_map/while/body/eval_jaxpr/ppermute | solution.py:13
  85.6 1.0 collective-permute-done.1
  87.5 5.2 %collective-permute-done.2 = f32[16]{0:T(128)S(1)} collective-permute-done((f32[16]{0:T(128)S(1)}, f32[16]{0:T(128)S(1)}, u32[]{:S(2)}, u32[]{:S(2)}) %collective-permute-start.2) | collective-permute-done | bytes 96 | tf_op jit(solution)/shard_map/while/body/eval_jaxpr/ppermute | solution.py:13
  92.7 1.0 collective-permute-done.1
  94.6 5.2 %collective-permute-done.2 = f32[16]{0:T(128)S(1)} collective-permute-done((f32[16]{0:T(128)S(1)}, f32[16]{0:T(128)S(1)}, u32[]{:S(2)}, u32[]{:S(2)}) %collective-permute-start.2) | collective-permute-done | bytes 96 | tf_op jit(solution)/shard_map/while/body/eval_jaxpr/ppermute | solution.py:13
  99.8 1.0 collective-permute-done.1
  101.7 5.2 %collective-permute-done.2 = f32[16]{0:T(128)S(1)} collective-permute-done((f32[16]{0:T(128)S(1)}, f32[16]{0:T(128)S(1)}, u32[]{:S(2)}, u32[]{:S(2)}) %collective-permute-start.2) | collective-permute-done | bytes 96 | tf_op jit(solution)/shard_map/while/body/eval_jaxpr/ppermute | solution.py:13
  107.0 1.0 collective-permute-done.1
  108.8 5.2 %collective-permute-done.2 = f32[16]{0:T(128)S(1)} collective-permute-done((f32[16]{0:T(128)S(1)}, f32[16]{0:T(128)S(1)}, u32[]{:S(2)}, u32[]{:S(2)}) %collective-permute-start.2) | collective-permute-done | bytes 96 | tf_op jit(solution)/shard_map/while/body/eval_jaxpr/ppermute | solution.py:13
  114.1 1.0 collective-permute-done.1
  116.0 5.2 %collective-permute-done.2 = f32[16]{0:T(128)S(1)} collective-permute-done((f32[16]{0:T(128)S(1)}, f32[16]{0:T(128)S(1)}, u32[]{:S(2)}, u32[]{:S(2)}) %collective-permute-start.2) | collective-permute-done | bytes 96 | tf_op jit(solution)/shard_map/while/body/eval_jaxpr/ppermute | solution.py:13
  121.2 1.0 collective-permute-done.1
  123.1 5.2 %collective-permute-done.2 = f32[16]{0:T(128)S(1)} collective-permute-done((f32[16]{0:T(128)S(1)}, f32[16]{0:T(128)S(1)}, u32[]{:S(2)}, u32[]{:S(2)}) %collective-permute-start.2) | collective-permute-done | bytes 96 | tf_op jit(solution)/shard_map/while/body/eval_jaxpr/ppermute | solution.py:13
  128.4 1.0 collective-permute-done.1
  130.2 5.2 %collective-permute-done.2 = f32[16]{0:T(128)S(1)} collective-permute-done((f32[16]{0:T(128)S(1)}, f32[16]{0:T(128)S(1)}, u32[]{:S(2)}, u32[]{:S(2)}) %collective-permute-start.2) | collective-permute-done | bytes 96 | tf_op jit(solution)/shard_map/while/body/eval_jaxpr/ppermute | solution.py:13
  137.4 5.2 %collective-permute-done.2 = f32[16]{0:T(128)S(1)} collective-permute-done((f32[16]{0:T(128)S(1)}, f32[16]{0:T(128)S(1)}, u32[]{:S(2)}, u32[]{:S(2)}) %collective-permute-start.2) | collective-permute-done | bytes 96 | tf_op jit(solution)/shard_map/while/body/eval_jaxpr/ppermute | solution.py:13
  142.6 1.0 collective-permute-done.1
  144.5 5.2 %collective-permute-done.2 = f32[16]{0:T(128)S(1)} collective-permute-done((f32[16]{0:T(128)S(1)}, f32[16]{0:T(128)S(1)}, u32[]{:S(2)}, u32[]{:S(2)}) %collective-permute-start.2) | collective-permute-done | bytes 96 | tf_op jit(solution)/shard_map/while/body/eval_jaxpr/ppermute | solution.py:13
  149.7 1.0 collective-permute-done.1
  151.6 5.2 %collective-permute-done.2 = f32[16]{0:T(128)S(1)} collective-permute-done((f32[16]{0:T(128)S(1)}, f32[16]{0:T(128)S(1)}, u32[]{:S(2)}, u32[]{:S(2)}) %collective-permute-start.2) | collective-permute-done | bytes 96 | tf_op jit(solution)/shard_map/while/body/eval_jaxpr/ppermute | solution.py:13
  158.8 5.2 %collective-permute-done.2 = f32[16]{0:T(128)S(1)} collective-permute-done((f32[16]{0:T(128)S(1)}, f32[16]{0:T(128)S(1)}, u32[]{:S(2)}, u32[]{:S(2)}) %collective-permute-start.2) | collective-permute-done | bytes 96 | tf_op jit(solution)/shard_map/while/body/eval_jaxpr/ppermute | solution.py:13
  164.0 1.0 collective-permute-done.1
  165.9 5.2 %collective-permute-done.2 = f32[16]{0:T(128)S(1)} collective-permute-done((f32[16]{0:T(128)S(1)}, f32[16]{0:T(128)S(1)}, u32[]{:S(2)}, u32[]{:S(2)}) %collective-permute-start.2) | collective-permute-done | bytes 96 | tf_op jit(solution)/shard_map/while/body/eval_jaxpr/ppermute | solution.py:13
  171.1 1.0 collective-permute-done.1
  173.0 5.2 %collective-permute-done.2 = f32[16]{0:T(128)S(1)} collective-permute-done((f32[16]{0:T(128)S(1)}, f32[16]{0:T(128)S(1)}, u32[]{:S(2)}, u32[]{:S(2)}) %collective-permute-start.2) | collective-permute-done | bytes 96 | tf_op jit(solution)/shard_map/while/body/eval_jaxpr/ppermute | solution.py:13
  180.0 6.4 %collective-permute-done.4 = f32[16,1152]{1,0:T(8,128)S(1)} collective-permute-done((f32[16,1152]{1,0:T(8,128)S(1)}, f32[16,1152]{1,0:T(8,128)S(1)}, u32[]{:S(2)}, u32[]{:S(2)}) %collective-permute-start.4) | collective-permute-done | bytes 73760 | tf_op jit(solution)/shard_map/ppermute | solution.py:13
  186.7 3.8 fusion.52
  190.5 5.5 %fusion.53 = f32[1152,2152]{0,1:T(8,128)} fusion(bf16[16,1152]{1,0:T(8,128)(2,1)S(1)} %multiply_convert_fusion.1, bf16[16,2152]{1,0:T(8,128)(2,1)S(1)} %multiply_reduce_fusion), kind=kOutput, calls=%fused_computation.86 | convolution fusion | flops 79331328 | bytes 10022144 | tf_op jit(solution)/shard_map/dot_general | solution.py:123
  195.9 4.1 mul.266
  200.0 9.5 %copy.18 = f32[1024,2152]{0,1:T(8,128)} copy(f32[1024,2152]{1,0:T(8,128)} %bitcast.31) | data formatting | bytes 17629184 | tf_op jit(solution)/shard_map/mul | solution.py:120
  209.5 17.1 %fusion.19 = f32[1152,2152]{0,1:T(8,128)} fusion(f32[1024,2152]{0,1:T(8,128)} %get-tuple-element.301, f32[1024,2152]{0,1:T(8,128)} %copy.18, f32[1024]{0:T(1024)S(1)} %div.49, bf16[1024,1152]{1,0:T(8,128)(2,1)} %param.8, f32[1024]{0:T(1024)S(1)} %add_rsqrt_fusion, f32[1024]{0:T(1024)S(1)} %broadcast_multiply_fusion), kind=kOutput, calls=%fused_computation.33 | convolution fusion | flops 5125996544 | bytes 29917184 | tf_op jit(solution)/shard_map/dot_general | solution.py:129
  226.7 11.5 %pad_maximum_fusion = f32[1152,4304]{0,1:T(8,128)} fusion(f32[1152,2152]{0,1:T(8,128)S(1)} %bitcast.30, f32[1152,2152]{0,1:T(8,128)} %fusion.19), kind=kLoop, calls=%fused_computation.18 | loop fusion | flops 4958208 | bytes 39665664 | tf_op jit(solution)/shard_map/concatenate | solution.py:127
  238.2 21.6 %copy.21 = f32[1152,4304]{1,0:T(8,128)} copy(f32[1152,4304]{0,1:T(8,128)} %pad_maximum_fusion) | data formatting | bytes 39665664
  260.9 4.6 collective-permute-done.3
  265.5 195.1 %reduce-scatter.4.cloned.1.call-done = f32[72,4304]{1,0:T(8,128)} async-done(((f32[1152,4304]{1,0:T(8,128)}), f32[72,4304]{1,0:T(8,128)}) %reduce-scatter.4.cloned.1.call-update) | async-done | bytes 1239568
  460.6 2.5 fusion.50
  (193 shorter events, 21.4 us)
Async XLA Ops:
  7.2 62.4 %all-reduce.2.cloned.1.call-start = ((), (), s32[]{:S(2)}) async-start(), calls=%async_computation.1 | async-start | bytes 147456 | tf_op jit(solution)/shard_map/psum | solution.py:77
  46.0 414.6 %reduce-scatter.4.cloned.1.call-start = ((), (), s32[]{:S(2)}) async-start(), calls=%async_computation.2 | async-start | bytes 21307392
  70.7 6.2 %collective-permute-start = (bf16[16,1152]{1,0:T(8,128)(2,1)S(1)}, bf16[16,1152]{1,0:T(8,128)(2,1)S(1)}, u32[]{:S(2)}, u32[]{:S(2)}) collective-permute-start(bf16[16,1152]{1,0:T(8,128)(2,1)S(1)} %copy.32), channel_id=1, source_target_pairs={{0,2},{2,4},{4,6},{6,8},{8,10},{10,12},{12,14},{14,16},{16,18},{18... | collective-permute-start | bytes 110600 | tf_op jit(solution)/shard_map/while/body/eval_jaxpr/ppermute | solution.py:13
  71.0 5.8 %collective-permute-start.2 = (f32[16]{0:T(128)S(1)}, f32[16]{0:T(128)S(1)}, u32[]{:S(2)}, u32[]{:S(2)}) collective-permute-start(f32[16]{0:T(128)S(1)} %multiply_add_fusion.4), channel_id=1, source_target_pairs={{0,2},{2,4},{4,6},{6,8},{8,10},{10,12},{12,14},{14,16},{16,18},{18... | collective-permute-start | bytes 200 | tf_op jit(solution)/shard_map/while/body/eval_jaxpr/ppermute | solution.py:13
  72.9 6.5 %collective-permute-start.1 = (f32[16,1152]{1,0:T(8,128)S(1)}, f32[16,1152]{1,0:T(8,128)S(1)}, u32[]{:S(2)}, u32[]{:S(2)}) collective-permute-start(f32[16,1152]{1,0:T(8,128)S(1)} %convolution_add_fusion.6), channel_id=1, source_target_pairs={{0,2},{2,4},{4,6},{6,8},{8,10},{10,12},{12,14},{14,16},{16,18},{18... | collective-permute-start | bytes 221192 | tf_op jit(solution)/shard_map/while/body/eval_jaxpr/ppermute | solution.py:13
  79.4 6.1 %collective-permute-start = (bf16[16,1152]{1,0:T(8,128)(2,1)S(1)}, bf16[16,1152]{1,0:T(8,128)(2,1)S(1)}, u32[]{:S(2)}, u32[]{:S(2)}) collective-permute-start(bf16[16,1152]{1,0:T(8,128)(2,1)S(1)} %copy.32), channel_id=1, source_target_pairs={{0,2},{2,4},{4,6},{6,8},{8,10},{10,12},{12,14},{14,16},{16,18},{18... | collective-permute-start | bytes 110600 | tf_op jit(solution)/shard_map/while/body/eval_jaxpr/ppermute | solution.py:13
  79.7 5.9 %collective-permute-start.2 = (f32[16]{0:T(128)S(1)}, f32[16]{0:T(128)S(1)}, u32[]{:S(2)}, u32[]{:S(2)}) collective-permute-start(f32[16]{0:T(128)S(1)} %multiply_add_fusion.4), channel_id=1, source_target_pairs={{0,2},{2,4},{4,6},{6,8},{8,10},{10,12},{12,14},{14,16},{16,18},{18... | collective-permute-start | bytes 200 | tf_op jit(solution)/shard_map/while/body/eval_jaxpr/ppermute | solution.py:13
  80.0 6.5 %collective-permute-start.1 = (f32[16,1152]{1,0:T(8,128)S(1)}, f32[16,1152]{1,0:T(8,128)S(1)}, u32[]{:S(2)}, u32[]{:S(2)}) collective-permute-start(f32[16,1152]{1,0:T(8,128)S(1)} %convolution_add_fusion.6), channel_id=1, source_target_pairs={{0,2},{2,4},{4,6},{6,8},{8,10},{10,12},{12,14},{14,16},{16,18},{18... | collective-permute-start | bytes 221192 | tf_op jit(solution)/shard_map/while/body/eval_jaxpr/ppermute | solution.py:13
  86.6 6.1 %collective-permute-start = (bf16[16,1152]{1,0:T(8,128)(2,1)S(1)}, bf16[16,1152]{1,0:T(8,128)(2,1)S(1)}, u32[]{:S(2)}, u32[]{:S(2)}) collective-permute-start(bf16[16,1152]{1,0:T(8,128)(2,1)S(1)} %copy.32), channel_id=1, source_target_pairs={{0,2},{2,4},{4,6},{6,8},{8,10},{10,12},{12,14},{14,16},{16,18},{18... | collective-permute-start | bytes 110600 | tf_op jit(solution)/shard_map/while/body/eval_jaxpr/ppermute | solution.py:13
  86.8 5.9 %collective-permute-start.2 = (f32[16]{0:T(128)S(1)}, f32[16]{0:T(128)S(1)}, u32[]{:S(2)}, u32[]{:S(2)}) collective-permute-start(f32[16]{0:T(128)S(1)} %multiply_add_fusion.4), channel_id=1, source_target_pairs={{0,2},{2,4},{4,6},{6,8},{8,10},{10,12},{12,14},{14,16},{16,18},{18... | collective-permute-start | bytes 200 | tf_op jit(solution)/shard_map/while/body/eval_jaxpr/ppermute | solution.py:13
  87.2 6.5 %collective-permute-start.1 = (f32[16,1152]{1,0:T(8,128)S(1)}, f32[16,1152]{1,0:T(8,128)S(1)}, u32[]{:S(2)}, u32[]{:S(2)}) collective-permute-start(f32[16,1152]{1,0:T(8,128)S(1)} %convolution_add_fusion.6), channel_id=1, source_target_pairs={{0,2},{2,4},{4,6},{6,8},{8,10},{10,12},{12,14},{14,16},{16,18},{18... | collective-permute-start | bytes 221192 | tf_op jit(solution)/shard_map/while/body/eval_jaxpr/ppermute | solution.py:13
  93.7 6.1 %collective-permute-start = (bf16[16,1152]{1,0:T(8,128)(2,1)S(1)}, bf16[16,1152]{1,0:T(8,128)(2,1)S(1)}, u32[]{:S(2)}, u32[]{:S(2)}) collective-permute-start(bf16[16,1152]{1,0:T(8,128)(2,1)S(1)} %copy.32), channel_id=1, source_target_pairs={{0,2},{2,4},{4,6},{6,8},{8,10},{10,12},{12,14},{14,16},{16,18},{18... | collective-permute-start | bytes 110600 | tf_op jit(solution)/shard_map/while/body/eval_jaxpr/ppermute | solution.py:13
  94.0 5.9 %collective-permute-start.2 = (f32[16]{0:T(128)S(1)}, f32[16]{0:T(128)S(1)}, u32[]{:S(2)}, u32[]{:S(2)}) collective-permute-start(f32[16]{0:T(128)S(1)} %multiply_add_fusion.4), channel_id=1, source_target_pairs={{0,2},{2,4},{4,6},{6,8},{8,10},{10,12},{12,14},{14,16},{16,18},{18... | collective-permute-start | bytes 200 | tf_op jit(solution)/shard_map/while/body/eval_jaxpr/ppermute | solution.py:13
  94.3 6.5 %collective-permute-start.1 = (f32[16,1152]{1,0:T(8,128)S(1)}, f32[16,1152]{1,0:T(8,128)S(1)}, u32[]{:S(2)}, u32[]{:S(2)}) collective-permute-start(f32[16,1152]{1,0:T(8,128)S(1)} %convolution_add_fusion.6), channel_id=1, source_target_pairs={{0,2},{2,4},{4,6},{6,8},{8,10},{10,12},{12,14},{14,16},{16,18},{18... | collective-permute-start | bytes 221192 | tf_op jit(solution)/shard_map/while/body/eval_jaxpr/ppermute | solution.py:13
  100.8 6.1 %collective-permute-start = (bf16[16,1152]{1,0:T(8,128)(2,1)S(1)}, bf16[16,1152]{1,0:T(8,128)(2,1)S(1)}, u32[]{:S(2)}, u32[]{:S(2)}) collective-permute-start(bf16[16,1152]{1,0:T(8,128)(2,1)S(1)} %copy.32), channel_id=1, source_target_pairs={{0,2},{2,4},{4,6},{6,8},{8,10},{10,12},{12,14},{14,16},{16,18},{18... | collective-permute-start | bytes 110600 | tf_op jit(solution)/shard_map/while/body/eval_jaxpr/ppermute | solution.py:13
  101.1 5.9 %collective-permute-start.2 = (f32[16]{0:T(128)S(1)}, f32[16]{0:T(128)S(1)}, u32[]{:S(2)}, u32[]{:S(2)}) collective-permute-start(f32[16]{0:T(128)S(1)} %multiply_add_fusion.4), channel_id=1, source_target_pairs={{0,2},{2,4},{4,6},{6,8},{8,10},{10,12},{12,14},{14,16},{16,18},{18... | collective-permute-start | bytes 200 | tf_op jit(solution)/shard_map/while/body/eval_jaxpr/ppermute | solution.py:13
  101.4 6.5 %collective-permute-start.1 = (f32[16,1152]{1,0:T(8,128)S(1)}, f32[16,1152]{1,0:T(8,128)S(1)}, u32[]{:S(2)}, u32[]{:S(2)}) collective-permute-start(f32[16,1152]{1,0:T(8,128)S(1)} %convolution_add_fusion.6), channel_id=1, source_target_pairs={{0,2},{2,4},{4,6},{6,8},{8,10},{10,12},{12,14},{14,16},{16,18},{18... | collective-permute-start | bytes 221192 | tf_op jit(solution)/shard_map/while/body/eval_jaxpr/ppermute | solution.py:13
  108.0 6.1 %collective-permute-start = (bf16[16,1152]{1,0:T(8,128)(2,1)S(1)}, bf16[16,1152]{1,0:T(8,128)(2,1)S(1)}, u32[]{:S(2)}, u32[]{:S(2)}) collective-permute-start(bf16[16,1152]{1,0:T(8,128)(2,1)S(1)} %copy.32), channel_id=1, source_target_pairs={{0,2},{2,4},{4,6},{6,8},{8,10},{10,12},{12,14},{14,16},{16,18},{18... | collective-permute-start | bytes 110600 | tf_op jit(solution)/shard_map/while/body/eval_jaxpr/ppermute | solution.py:13
  108.2 5.9 %collective-permute-start.2 = (f32[16]{0:T(128)S(1)}, f32[16]{0:T(128)S(1)}, u32[]{:S(2)}, u32[]{:S(2)}) collective-permute-start(f32[16]{0:T(128)S(1)} %multiply_add_fusion.4), channel_id=1, source_target_pairs={{0,2},{2,4},{4,6},{6,8},{8,10},{10,12},{12,14},{14,16},{16,18},{18... | collective-permute-start | bytes 200 | tf_op jit(solution)/shard_map/while/body/eval_jaxpr/ppermute | solution.py:13
  108.5 6.5 %collective-permute-start.1 = (f32[16,1152]{1,0:T(8,128)S(1)}, f32[16,1152]{1,0:T(8,128)S(1)}, u32[]{:S(2)}, u32[]{:S(2)}) collective-permute-start(f32[16,1152]{1,0:T(8,128)S(1)} %convolution_add_fusion.6), channel_id=1, source_target_pairs={{0,2},{2,4},{4,6},{6,8},{8,10},{10,12},{12,14},{14,16},{16,18},{18... | collective-permute-start | bytes 221192 | tf_op jit(solution)/shard_map/while/body/eval_jaxpr/ppermute | solution.py:13
  115.1 6.1 %collective-permute-start = (bf16[16,1152]{1,0:T(8,128)(2,1)S(1)}, bf16[16,1152]{1,0:T(8,128)(2,1)S(1)}, u32[]{:S(2)}, u32[]{:S(2)}) collective-permute-start(bf16[16,1152]{1,0:T(8,128)(2,1)S(1)} %copy.32), channel_id=1, source_target_pairs={{0,2},{2,4},{4,6},{6,8},{8,10},{10,12},{12,14},{14,16},{16,18},{18... | collective-permute-start | bytes 110600 | tf_op jit(solution)/shard_map/while/body/eval_jaxpr/ppermute | solution.py:13
  115.3 5.9 %collective-permute-start.2 = (f32[16]{0:T(128)S(1)}, f32[16]{0:T(128)S(1)}, u32[]{:S(2)}, u32[]{:S(2)}) collective-permute-start(f32[16]{0:T(128)S(1)} %multiply_add_fusion.4), channel_id=1, source_target_pairs={{0,2},{2,4},{4,6},{6,8},{8,10},{10,12},{12,14},{14,16},{16,18},{18... | collective-permute-start | bytes 200 | tf_op jit(solution)/shard_map/while/body/eval_jaxpr/ppermute | solution.py:13
  115.7 6.5 %collective-permute-start.1 = (f32[16,1152]{1,0:T(8,128)S(1)}, f32[16,1152]{1,0:T(8,128)S(1)}, u32[]{:S(2)}, u32[]{:S(2)}) collective-permute-start(f32[16,1152]{1,0:T(8,128)S(1)} %convolution_add_fusion.6), channel_id=1, source_target_pairs={{0,2},{2,4},{4,6},{6,8},{8,10},{10,12},{12,14},{14,16},{16,18},{18... | collective-permute-start | bytes 221192 | tf_op jit(solution)/shard_map/while/body/eval_jaxpr/ppermute | solution.py:13
  122.2 6.1 %collective-permute-start = (bf16[16,1152]{1,0:T(8,128)(2,1)S(1)}, bf16[16,1152]{1,0:T(8,128)(2,1)S(1)}, u32[]{:S(2)}, u32[]{:S(2)}) collective-permute-start(bf16[16,1152]{1,0:T(8,128)(2,1)S(1)} %copy.32), channel_id=1, source_target_pairs={{0,2},{2,4},{4,6},{6,8},{8,10},{10,12},{12,14},{14,16},{16,18},{18... | collective-permute-start | bytes 110600 | tf_op jit(solution)/shard_map/while/body/eval_jaxpr/ppermute | solution.py:13
  122.5 5.9 %collective-permute-start.2 = (f32[16]{0:T(128)S(1)}, f32[16]{0:T(128)S(1)}, u32[]{:S(2)}, u32[]{:S(2)}) collective-permute-start(f32[16]{0:T(128)S(1)} %multiply_add_fusion.4), channel_id=1, source_target_pairs={{0,2},{2,4},{4,6},{6,8},{8,10},{10,12},{12,14},{14,16},{16,18},{18... | collective-permute-start | bytes 200 | tf_op jit(solution)/shard_map/while/body/eval_jaxpr/ppermute | solution.py:13
  122.8 6.5 %collective-permute-start.1 = (f32[16,1152]{1,0:T(8,128)S(1)}, f32[16,1152]{1,0:T(8,128)S(1)}, u32[]{:S(2)}, u32[]{:S(2)}) collective-permute-start(f32[16,1152]{1,0:T(8,128)S(1)} %convolution_add_fusion.6), channel_id=1, source_target_pairs={{0,2},{2,4},{4,6},{6,8},{8,10},{10,12},{12,14},{14,16},{16,18},{18... | collective-permute-start | bytes 221192 | tf_op jit(solution)/shard_map/while/body/eval_jaxpr/ppermute | solution.py:13
  129.3 6.1 %collective-permute-start = (bf16[16,1152]{1,0:T(8,128)(2,1)S(1)}, bf16[16,1152]{1,0:T(8,128)(2,1)S(1)}, u32[]{:S(2)}, u32[]{:S(2)}) collective-permute-start(bf16[16,1152]{1,0:T(8,128)(2,1)S(1)} %copy.32), channel_id=1, source_target_pairs={{0,2},{2,4},{4,6},{6,8},{8,10},{10,12},{12,14},{14,16},{16,18},{18... | collective-permute-start | bytes 110600 | tf_op jit(solution)/shard_map/while/body/eval_jaxpr/ppermute | solution.py:13
  129.6 5.9 %collective-permute-start.2 = (f32[16]{0:T(128)S(1)}, f32[16]{0:T(128)S(1)}, u32[]{:S(2)}, u32[]{:S(2)}) collective-permute-start(f32[16]{0:T(128)S(1)} %multiply_add_fusion.4), channel_id=1, source_target_pairs={{0,2},{2,4},{4,6},{6,8},{8,10},{10,12},{12,14},{14,16},{16,18},{18... | collective-permute-start | bytes 200 | tf_op jit(solution)/shard_map/while/body/eval_jaxpr/ppermute | solution.py:13
  129.9 6.5 %collective-permute-start.1 = (f32[16,1152]{1,0:T(8,128)S(1)}, f32[16,1152]{1,0:T(8,128)S(1)}, u32[]{:S(2)}, u32[]{:S(2)}) collective-permute-start(f32[16,1152]{1,0:T(8,128)S(1)} %convolution_add_fusion.6), channel_id=1, source_target_pairs={{0,2},{2,4},{4,6},{6,8},{8,10},{10,12},{12,14},{14,16},{16,18},{18... | collective-permute-start | bytes 221192 | tf_op jit(solution)/shard_map/while/body/eval_jaxpr/ppermute | solution.py:13
  136.5 6.1 %collective-permute-start = (bf16[16,1152]{1,0:T(8,128)(2,1)S(1)}, bf16[16,1152]{1,0:T(8,128)(2,1)S(1)}, u32[]{:S(2)}, u32[]{:S(2)}) collective-permute-start(bf16[16,1152]{1,0:T(8,128)(2,1)S(1)} %copy.32), channel_id=1, source_target_pairs={{0,2},{2,4},{4,6},{6,8},{8,10},{10,12},{12,14},{14,16},{16,18},{18... | collective-permute-start | bytes 110600 | tf_op jit(solution)/shard_map/while/body/eval_jaxpr/ppermute | solution.py:13
  136.7 5.9 %collective-permute-start.2 = (f32[16]{0:T(128)S(1)}, f32[16]{0:T(128)S(1)}, u32[]{:S(2)}, u32[]{:S(2)}) collective-permute-start(f32[16]{0:T(128)S(1)} %multiply_add_fusion.4), channel_id=1, source_target_pairs={{0,2},{2,4},{4,6},{6,8},{8,10},{10,12},{12,14},{14,16},{16,18},{18... | collective-permute-start | bytes 200 | tf_op jit(solution)/shard_map/while/body/eval_jaxpr/ppermute | solution.py:13
  137.1 6.5 %collective-permute-start.1 = (f32[16,1152]{1,0:T(8,128)S(1)}, f32[16,1152]{1,0:T(8,128)S(1)}, u32[]{:S(2)}, u32[]{:S(2)}) collective-permute-start(f32[16,1152]{1,0:T(8,128)S(1)} %convolution_add_fusion.6), channel_id=1, source_target_pairs={{0,2},{2,4},{4,6},{6,8},{8,10},{10,12},{12,14},{14,16},{16,18},{18... | collective-permute-start | bytes 221192 | tf_op jit(solution)/shard_map/while/body/eval_jaxpr/ppermute | solution.py:13
  143.6 6.1 %collective-permute-start = (bf16[16,1152]{1,0:T(8,128)(2,1)S(1)}, bf16[16,1152]{1,0:T(8,128)(2,1)S(1)}, u32[]{:S(2)}, u32[]{:S(2)}) collective-permute-start(bf16[16,1152]{1,0:T(8,128)(2,1)S(1)} %copy.32), channel_id=1, source_target_pairs={{0,2},{2,4},{4,6},{6,8},{8,10},{10,12},{12,14},{14,16},{16,18},{18... | collective-permute-start | bytes 110600 | tf_op jit(solution)/shard_map/while/body/eval_jaxpr/ppermute | solution.py:13
  143.9 5.9 %collective-permute-start.2 = (f32[16]{0:T(128)S(1)}, f32[16]{0:T(128)S(1)}, u32[]{:S(2)}, u32[]{:S(2)}) collective-permute-start(f32[16]{0:T(128)S(1)} %multiply_add_fusion.4), channel_id=1, source_target_pairs={{0,2},{2,4},{4,6},{6,8},{8,10},{10,12},{12,14},{14,16},{16,18},{18... | collective-permute-start | bytes 200 | tf_op jit(solution)/shard_map/while/body/eval_jaxpr/ppermute | solution.py:13
  144.2 6.5 %collective-permute-start.1 = (f32[16,1152]{1,0:T(8,128)S(1)}, f32[16,1152]{1,0:T(8,128)S(1)}, u32[]{:S(2)}, u32[]{:S(2)}) collective-permute-start(f32[16,1152]{1,0:T(8,128)S(1)} %convolution_add_fusion.6), channel_id=1, source_target_pairs={{0,2},{2,4},{4,6},{6,8},{8,10},{10,12},{12,14},{14,16},{16,18},{18... | collective-permute-start | bytes 221192 | tf_op jit(solution)/shard_map/while/body/eval_jaxpr/ppermute | solution.py:13
  150.7 6.1 %collective-permute-start = (bf16[16,1152]{1,0:T(8,128)(2,1)S(1)}, bf16[16,1152]{1,0:T(8,128)(2,1)S(1)}, u32[]{:S(2)}, u32[]{:S(2)}) collective-permute-start(bf16[16,1152]{1,0:T(8,128)(2,1)S(1)} %copy.32), channel_id=1, source_target_pairs={{0,2},{2,4},{4,6},{6,8},{8,10},{10,12},{12,14},{14,16},{16,18},{18... | collective-permute-start | bytes 110600 | tf_op jit(solution)/shard_map/while/body/eval_jaxpr/ppermute | solution.py:13
  151.0 5.9 %collective-permute-start.2 = (f32[16]{0:T(128)S(1)}, f32[16]{0:T(128)S(1)}, u32[]{:S(2)}, u32[]{:S(2)}) collective-permute-start(f32[16]{0:T(128)S(1)} %multiply_add_fusion.4), channel_id=1, source_target_pairs={{0,2},{2,4},{4,6},{6,8},{8,10},{10,12},{12,14},{14,16},{16,18},{18... | collective-permute-start | bytes 200 | tf_op jit(solution)/shard_map/while/body/eval_jaxpr/ppermute | solution.py:13
  151.3 6.5 %collective-permute-start.1 = (f32[16,1152]{1,0:T(8,128)S(1)}, f32[16,1152]{1,0:T(8,128)S(1)}, u32[]{:S(2)}, u32[]{:S(2)}) collective-permute-start(f32[16,1152]{1,0:T(8,128)S(1)} %convolution_add_fusion.6), channel_id=1, source_target_pairs={{0,2},{2,4},{4,6},{6,8},{8,10},{10,12},{12,14},{14,16},{16,18},{18... | collective-permute-start | bytes 221192 | tf_op jit(solution)/shard_map/while/body/eval_jaxpr/ppermute | solution.py:13
  157.9 6.1 %collective-permute-start = (bf16[16,1152]{1,0:T(8,128)(2,1)S(1)}, bf16[16,1152]{1,0:T(8,128)(2,1)S(1)}, u32[]{:S(2)}, u32[]{:S(2)}) collective-permute-start(bf16[16,1152]{1,0:T(8,128)(2,1)S(1)} %copy.32), channel_id=1, source_target_pairs={{0,2},{2,4},{4,6},{6,8},{8,10},{10,12},{12,14},{14,16},{16,18},{18... | collective-permute-start | bytes 110600 | tf_op jit(solution)/shard_map/while/body/eval_jaxpr/ppermute | solution.py:13
  158.1 5.9 %collective-permute-start.2 = (f32[16]{0:T(128)S(1)}, f32[16]{0:T(128)S(1)}, u32[]{:S(2)}, u32[]{:S(2)}) collective-permute-start(f32[16]{0:T(128)S(1)} %multiply_add_fusion.4), channel_id=1, source_target_pairs={{0,2},{2,4},{4,6},{6,8},{8,10},{10,12},{12,14},{14,16},{16,18},{18... | collective-permute-start | bytes 200 | tf_op jit(solution)/shard_map/while/body/eval_jaxpr/ppermute | solution.py:13
  158.5 6.5 %collective-permute-start.1 = (f32[16,1152]{1,0:T(8,128)S(1)}, f32[16,1152]{1,0:T(8,128)S(1)}, u32[]{:S(2)}, u32[]{:S(2)}) collective-permute-start(f32[16,1152]{1,0:T(8,128)S(1)} %convolution_add_fusion.6), channel_id=1, source_target_pairs={{0,2},{2,4},{4,6},{6,8},{8,10},{10,12},{12,14},{14,16},{16,18},{18... | collective-permute-start | bytes 221192 | tf_op jit(solution)/shard_map/while/body/eval_jaxpr/ppermute | solution.py:13
  165.0 6.1 %collective-permute-start = (bf16[16,1152]{1,0:T(8,128)(2,1)S(1)}, bf16[16,1152]{1,0:T(8,128)(2,1)S(1)}, u32[]{:S(2)}, u32[]{:S(2)}) collective-permute-start(bf16[16,1152]{1,0:T(8,128)(2,1)S(1)} %copy.32), channel_id=1, source_target_pairs={{0,2},{2,4},{4,6},{6,8},{8,10},{10,12},{12,14},{14,16},{16,18},{18... | collective-permute-start | bytes 110600 | tf_op jit(solution)/shard_map/while/body/eval_jaxpr/ppermute | solution.py:13
  165.2 5.9 %collective-permute-start.2 = (f32[16]{0:T(128)S(1)}, f32[16]{0:T(128)S(1)}, u32[]{:S(2)}, u32[]{:S(2)}) collective-permute-start(f32[16]{0:T(128)S(1)} %multiply_add_fusion.4), channel_id=1, source_target_pairs={{0,2},{2,4},{4,6},{6,8},{8,10},{10,12},{12,14},{14,16},{16,18},{18... | collective-permute-start | bytes 200 | tf_op jit(solution)/shard_map/while/body/eval_jaxpr/ppermute | solution.py:13
  165.6 6.5 %collective-permute-start.1 = (f32[16,1152]{1,0:T(8,128)S(1)}, f32[16,1152]{1,0:T(8,128)S(1)}, u32[]{:S(2)}, u32[]{:S(2)}) collective-permute-start(f32[16,1152]{1,0:T(8,128)S(1)} %convolution_add_fusion.6), channel_id=1, source_target_pairs={{0,2},{2,4},{4,6},{6,8},{8,10},{10,12},{12,14},{14,16},{16,18},{18... | collective-permute-start | bytes 221192 | tf_op jit(solution)/shard_map/while/body/eval_jaxpr/ppermute | solution.py:13
  172.1 6.1 %collective-permute-start = (bf16[16,1152]{1,0:T(8,128)(2,1)S(1)}, bf16[16,1152]{1,0:T(8,128)(2,1)S(1)}, u32[]{:S(2)}, u32[]{:S(2)}) collective-permute-start(bf16[16,1152]{1,0:T(8,128)(2,1)S(1)} %copy.32), channel_id=1, source_target_pairs={{0,2},{2,4},{4,6},{6,8},{8,10},{10,12},{12,14},{14,16},{16,18},{18... | collective-permute-start | bytes 110600 | tf_op jit(solution)/shard_map/while/body/eval_jaxpr/ppermute | solution.py:13
  172.4 5.9 %collective-permute-start.2 = (f32[16]{0:T(128)S(1)}, f32[16]{0:T(128)S(1)}, u32[]{:S(2)}, u32[]{:S(2)}) collective-permute-start(f32[16]{0:T(128)S(1)} %multiply_add_fusion.4), channel_id=1, source_target_pairs={{0,2},{2,4},{4,6},{6,8},{8,10},{10,12},{12,14},{14,16},{16,18},{18... | collective-permute-start | bytes 200 | tf_op jit(solution)/shard_map/while/body/eval_jaxpr/ppermute | solution.py:13
  172.7 6.5 %collective-permute-start.1 = (f32[16,1152]{1,0:T(8,128)S(1)}, f32[16,1152]{1,0:T(8,128)S(1)}, u32[]{:S(2)}, u32[]{:S(2)}) collective-permute-start(f32[16,1152]{1,0:T(8,128)S(1)} %convolution_add_fusion.6), channel_id=1, source_target_pairs={{0,2},{2,4},{4,6},{6,8},{8,10},{10,12},{12,14},{14,16},{16,18},{18... | collective-permute-start | bytes 221192 | tf_op jit(solution)/shard_map/while/body/eval_jaxpr/ppermute | solution.py:13
  179.7 6.7 %collective-permute-start.4 = (f32[16,1152]{1,0:T(8,128)S(1)}, f32[16,1152]{1,0:T(8,128)S(1)}, u32[]{:S(2)}, u32[]{:S(2)}) collective-permute-start(f32[16,1152]{1,0:T(8,128)S(1)} %convolution_add_fusion.2), channel_id=1, source_target_pairs={{0,2},{2,4},{4,6},{6,8},{8,10},{10,12},{12,14},{14,16},{16,18},{18... | collective-permute-start | bytes 221192 | tf_op jit(solution)/shard_map/ppermute | solution.py:13
  (7 other events, 95.1 us)
Sparse Core Ops, SparseCore 0:
  46.1 23.3 all-reduce.1
  259.9 200.6 reduce-scatter.3
where the time goes:
time: 472 us; the launch traced here: 470 us
  waiting for transfers between devices  322 us (68%)
  matrix products  55.4 us (12%)
  local copies, waits for them, and re-layouts  48.7 us (10%)
  other arithmetic  25.7 us (5%)
  between operations  14.2 us (3%)
    unnamed x3, waiting for transfers between devices  195 us
    ppermute x47, waiting for transfers between devices, passed_along(): return lax.ppermute(value, axis, pairs)  104 us
    psum x1, waiting for transfers between devices, on_device(): pooled = tmean + lax.psum(partial_value, 'mp')  22.2 us
    unnamed x14, local copies, waits for them, and re-layouts  22.1 us
    dot_general x1, matrix products, on_device(): lax.dot_general(normed, pre_grad, (((0,), (0,)), ((), ())), preferred_ele...  17.1 us
    dot_general x1, matrix products, on_device(): pre = jnp.dot(normed, w_up, preferred_element_type=jnp.float32)  14.8 us
    mul x2, local copies, waits for them, and re-layouts, on_device(): share[:, :, None] * hidden_grad[:, None, :]  13.6 us
    concatenate x1, other arithmetic, on_device(): jnp.concatenate([lax.dot_general(normed, pre_grad, (((0,), (0,)), ((), ()...  11.5 us
  transfers between devices with their start and end apart: 49, of which 34 were waited for; matrix products, arithmetic and copies ran while one was open for 3% of the time, Pallas kernels for 0%

commit v1 on v0

v1 whole, which is shorter than its diff:
```python
import jax
import jax.numpy as jnp
from jax import lax
from jax.sharding import PartitionSpec as P

LOGIT_SCALE = 117.0
LOGIT_SHIFT = -12.9


def layer_norm(rows):
    center = rows - jnp.mean(rows, -1, keepdims=True)
    spread = jnp.mean(center * center, -1, keepdims=True)
    return center * lax.rsqrt(spread + 1e-06)


def gelu_pair(pre):
    const = 0.7978845608028654
    inner = const * (pre + 0.044715 * pre * pre * pre)
    tanh_u = jnp.tanh(inner)
    value = 0.5 * pre * (1.0 + tanh_u)
    slope = 0.5 * (1.0 + tanh_u) + 0.5 * pre * (1.0 - tanh_u * tanh_u) * const * (
        1.0 + 3.0 * 0.044715 * pre * pre
    )
    return (value, slope)


def unit_rows(rows):
    scale = lax.rsqrt(jnp.sum(rows * rows, 1, keepdims=True) + 1e-06)
    return (rows * scale, scale)


def signed_logits(text_rows, text_group, image_rows, image_group):
    logits = (
        LOGIT_SCALE
        * lax.dot_general(
            text_rows, image_rows, (((1,), (1,)), ((), ())), preferred_element_type=jnp.float32
        )
        + LOGIT_SHIFT
    )
    signs = jnp.where(text_group[:, None] == image_group[None, :], 1.0, -1.0).astype(jnp.float32)
    return (signs, signs * logits)


def loss_slope(signs, signed):
    return (-LOGIT_SCALE * signs * jax.nn.sigmoid(-signed)).astype(jnp.bfloat16)


def through_unit(back, unit, scale):
    return (back - unit * jnp.sum(unit * back, 1, keepdims=True)) * scale


def on_device(tokens, lengths, images, pair_group, w_up, w_down):
    captions = lengths.shape[0]
    seq_len = tokens.shape[0] // captions
    width = tokens.shape[1]
    hidden = w_up.shape[1]
    devices = lax.axis_size("dp")
    own_index = lax.axis_index("dp")
    total = captions * devices
    own_rows = width // devices
    own_group = lax.dynamic_slice_in_dim(pair_group, own_index * captions, captions)

    unit_image, image_scale = unit_rows(images.astype(jnp.float32))
    image_half = unit_image.astype(jnp.bfloat16)
    all_images = lax.all_gather(image_half, "dp", axis=0, tiled=True)

    tok_float = tokens.astype(jnp.float32)
    normed = layer_norm(tok_float).astype(jnp.bfloat16)
    pre = jnp.dot(normed, w_up, preferred_element_type=jnp.float32)
    value, slope = gelu_pair(pre)
    position = jnp.arange(seq_len, dtype=jnp.int32)
    valid = (position[None, :] < lengths[:, None]).astype(jnp.float32)
    share = valid / jnp.sum(valid, 1, keepdims=True)
    gmean = jnp.sum(value.reshape(captions, seq_len, hidden) * share[:, :, None], 1)
    tmean = jnp.sum(tok_float.reshape(captions, seq_len, width) * share[:, :, None], 1)
    gbar = gmean.astype(jnp.bfloat16)
    partial_value = lax.dot_general(
        gbar, w_down, (((1,), (1,)), ((), ())), preferred_element_type=jnp.float32
    )
    pooled = tmean + lax.psum(partial_value, "mp")
    unit_text, text_scale = unit_rows(pooled)
    text_half = unit_text.astype(jnp.bfloat16)

    signs, signed = signed_logits(text_half, own_group, all_images, pair_group)
    caption_loss = -jnp.sum(jax.nn.log_sigmoid(signed), 1) / total
    text_back = jnp.dot(loss_slope(signs, signed), all_images, preferred_element_type=jnp.float32)
    pooled_half = through_unit(text_back, unit_text, text_scale).astype(jnp.bfloat16)

    hidden_grad = jnp.dot(pooled_half, w_down, preferred_element_type=jnp.float32)
    pre_grad = (
        share[:, :, None] * hidden_grad[:, None, :] * slope.reshape(captions, seq_len, hidden)
    ).astype(jnp.bfloat16)
    pre_grad = pre_grad.reshape(captions * seq_len, hidden)
    up_grad = lax.psum_scatter(
        lax.dot_general(
            normed, pre_grad, (((0,), (0,)), ((), ())), preferred_element_type=jnp.float32
        ),
        "dp",
        scatter_dimension=0,
        tiled=True,
    )

    all_texts = lax.all_gather(text_half, "dp", axis=0, tiled=True)
    signs, signed = signed_logits(all_texts, pair_group, image_half, own_group)
    image_back = lax.dot_general(
        loss_slope(signs, signed), all_texts, (((0,), (0,)), ((), ())),
        preferred_element_type=jnp.float32,
    )
    image_grad = through_unit(image_back, unit_image, image_scale)
    all_gbar = lax.all_gather(gbar, "dp", axis=0, tiled=True)
    all_pooled = lax.all_gather(pooled_half, "dp", axis=0, tiled=True)
    own_pooled = lax.dynamic_slice_in_dim(all_pooled, own_index * own_rows, own_rows, 1)
    down_grad = lax.dot_general(
        own_pooled, all_gbar, (((0,), (0,)), ((), ())), preferred_element_type=jnp.float32
    )
    return (caption_loss, image_grad, up_grad, down_grad)


def solution(mesh):
    in_specs = (P("dp", None), P("dp"), P("dp", None), P(), P(None, "mp"), P(None, "mp"))
    out_specs = (P("dp"), P("dp", None), P("dp", "mp"), P("dp", "mp"))
    return jax.shard_map(
        on_device, mesh=mesh, in_specs=in_specs, out_specs=out_specs, check_vma=False
    )
```

time: 472 us -> 230 us (0.49)
  waiting for transfers between devices: 322 us -> 69.1 us
  blocking collectives: 0 us -> 66.5 us
  local copies, waits for them, and re-layouts: 48.7 us -> 22.9 us
  matrix products: 55.4 us -> 42.1 us
  other arithmetic: 25.7 us -> 13.2 us
    unnamed x3 -> x4, waiting for transfers between devices: 195 us -> 69.1 us
    ppermute x47 -> x0, waiting for transfers between devices: 104 us -> none  [passed_along(): return lax.ppermute(value, axis, pairs)]
    all_gather x0 -> x3, blocking collectives: none -> 66.5 us  [the longest x1 25.2 us: on_device(): all_images = lax.all_gather(image_half, 'dp', axis=0, tiled=True)]
    psum x1, waiting for transfers between devices: 22.2 us -> 0.01 us  [on_device(): pooled = tmean + lax.psum(partial_value, 'mp')]
    unnamed x14 -> x10, local copies, waits for them, and re-layouts: 22.1 us -> 0.02 us
    dot_general x49 -> x4, matrix products: 15.9 us -> 3.99 us  [the longest x1 2.49 us: on_device(): lax.dot_general(own_pooled, all_gbar, (((0,), (0,)), ((), ())), preferred...]
    concatenate x1 -> x0, other arithmetic: 11.5 us -> none  [on_device(): jnp.concatenate([lax.dot_general(normed, pre_grad, (((0,), (0,)), ((), ()...]
  transfers between devices with their start and end apart: 49 -> 3, of which waited for: 34 -> 1; matrix products, arithmetic and copies ran while one was open for 3% -> 18% of each run, Pallas kernels for 0% -> 0%
where the time goes in v1:
time: 230 us; the launch traced here: 229 us
  waiting for transfers between devices  69.1 us (30%)
  blocking collectives  66.5 us (29%)
  matrix products  42.1 us (18%)
  local copies, waits for them, and re-layouts  22.9 us (10%)
  between operations  15.6 us (7%)
  other arithmetic  13.2 us (6%)
    unnamed x4, waiting for transfers between devices  69.1 us
    all_gather x1, blocking collectives, on_device(): all_images = lax.all_gather(image_half, 'dp', axis=0, tiled=True)  25.2 us
    all_gather x1, blocking collectives, on_device(): all_pooled = lax.all_gather(pooled_half, 'dp', axis=0, tiled=True)  22.1 us
    all_gather x1, blocking collectives, on_device(): all_texts = lax.all_gather(text_half, 'dp', axis=0, tiled=True)  19.2 us
    dot_general x1, matrix products, on_device(): lax.dot_general(normed, pre_grad, (((0,), (0,)), ((), ())), preferred_ele...  15.5 us
    dot_general x1, matrix products, on_device(): pre = jnp.dot(normed, w_up, preferred_element_type=jnp.float32)  14.8 us
    mul x2, local copies, waits for them, and re-layouts, on_device(): share[:, :, None] * hidden_grad[:, None, :]  13.5 us
    mul x1, local copies, waits for them, and re-layouts, gelu_pair(): value = 0.5 * pre * (1.0 + tanh_u)  9.24 us
  transfers between devices with their start and end apart: 3, of which 1 were waited for; matrix products, arithmetic and copies ran while one was open for 18% of the time, Pallas kernels for 0%

profile of v1, /device:TPU:0, one launch (start us, length us, event | category | flops | bytes accessed | tf_op | source)
XLA Modules:
  0.0 229.4 jit_solution(9921411807161620111)
XLA Ops:
  8.0 0.0 all-reduce.3.cloned.1.call-start
  8.0 2.0 convert_reduce_fusion
  10.1 2.4 %multiply_reduce_fusion.1 = f32[1024]{0:T(1024)S(1)} fusion(bf16[1024,1152]{1,0:T(8,128)(2,1)} %param.6, f32[1024]{0:T(1024)S(1)} %broadcast_multiply_fusion), kind=kLoop, calls=%fused_computation.12 | loop fusion | flops 4717568 | bytes 2367488 | tf_op jit(solution)/shard_map/reduce_sum | solution.py:12
  12.5 14.8 %add_multiply_fusion = (f32[1024,2152]{0,1:T(8,128)}, f32[1024,2152]{0,1:T(8,128)}) fusion(bf16[1152,2152]{0,1:T(8,128)(2,1)} %param.10, bf16[1024,1152]{1,0:T(8,128)(2,1)} %param.6, f32[1024]{0:T(1024)S(1)} %add_rsqrt_fusion, f32[1024]{0:T(1024)S(1)} %broadcast_multiply_fusion), kind=kOutput, calls=%fused_computation.10 | convolution fusion | flops 5099552768 | bytes 24954880 | tf_op jit(solution)/shard_map/dot_general | solution.py:69
  27.4 0.0 copy-start.4
  27.4 9.2 %copy.13 = f32[1024,2152]{1,0:T(8,128)} copy(f32[1024,2152]{0,1:T(8,128)} %get-tuple-element.6) | data formatting | bytes 17629184 | tf_op jit(solution)/shard_map/mul | solution.py:20
  36.6 0.0 copy-done.4
  36.6 0.0 copy-start
  36.6 0.0 copy-start.2
  36.6 0.0 copy-start.3
  36.6 0.2 convert_reduce_fusion.1
  36.8 0.1 convert_divide_fusion
  36.9 4.9 %multiply_reduce_fusion = bf16[16,2152]{1,0:T(8,128)(2,1)S(1)} fusion(f32[16,64]{1,0:T(8,128)S(1)} %convert_divide_fusion, f32[1024,2152]{1,0:T(8,128)} %copy.13), kind=kLoop, calls=%fused_computation.2 | loop fusion | flops 4372864 | bytes 8887552 | tf_op jit(solution)/shard_map/reduce_sum | solution.py:74
  41.8 0.0 copy-start.1
  41.8 3.8 %fusion.64 = f32[16,1152]{1,0:T(8,128)} fusion(bf16[16,2152]{1,0:T(8,128)(2,1)S(1)} %multiply_reduce_fusion, bf16[1152,2152]{0,1:T(8,128)(2,1)} %param.11), kind=kOutput, calls=%fused_computation.87 | convolution fusion | flops 79331328 | bytes 5100800 | tf_op jit(solution)/shard_map/dot_general | solution.py:77
  45.6 0.0 all-reduce.3.cloned.1.call-update
  45.6 0.0 all-gather.2.cloned.1.call-start
  45.7 0.0 copy-done.1
  45.7 0.5 all-gather.2.cloned.1.call-update
  46.2 0.0 reduce-scatter.4.cloned.1.call-start
  46.3 0.0 copy-done
  46.3 1.0 multiply_reduce_fusion.2
  47.3 0.1 div.37
  47.3 0.0 copy-done.2
  47.3 0.1 fusion.25
  47.5 0.1 fusion.21
  47.5 25.2 %all_gather.12 = bf16[256,1152]{1,0:T(8,128)(2,1)S(1)} all-gather(bf16[16,1152]{1,0:T(8,128)(2,1)S(1)} %fusion.21), channel_id=1, replica_groups=mesh['dp'=16,'mp'=2] {'dp'}, dimensions={0}, use_global_device_ids=true | all-gather | bytes 626688 | tf_op jit(solution)/shard_map/all_gather | solution.py:65
  72.7 0.0 copy-done.3
  72.7 0.1 dynamic_slice.6
  72.8 0.0 all-reduce.3.cloned.1.call-done
  72.8 1.0 multiply_reduce_fusion.4
  73.8 0.1 multiply_convert_fusion.2
  73.9 0.4 fusion.32
  74.3 0.4 multiply_reduce_fusion.3
  74.7 0.1 multiply_convert_fusion.1
  74.8 3.9 %fusion.65 = f32[16,2152]{1,0:T(8,128)S(1)} fusion(bf16[16,1152]{1,0:T(8,128)(2,1)S(1)} %multiply_convert_fusion.1, bf16[1152,2152]{0,1:T(8,128)(2,1)} %param.11), kind=kOutput, calls=%fused_computation.88 | convolution fusion | flops 79331328 | bytes 5132800 | tf_op jit(solution)/shard_map/dot_general | solution.py:89
  78.7 4.0 %mul.233 = f32[16,64,2152]{2,1,0:T(8,128)} broadcast(f32[16,2152]{1,0:T(8,128)S(1)} %fusion.65), dimensions={0,2} | broadcast | bytes 8952320 | tf_op jit(solution)/shard_map/mul | solution.py:91
  82.7 9.5 %copy.14 = f32[1024,2152]{0,1:T(8,128)} copy(f32[1024,2152]{1,0:T(8,128)} %bitcast.17) | data formatting | bytes 17629184 | tf_op jit(solution)/shard_map/mul | solution.py:91
  92.2 15.5 %fusion.7 = f32[1152,2152]{1,0:T(8,128)} fusion(f32[1024,2152]{0,1:T(8,128)} %get-tuple-element.7, f32[1024,2152]{0,1:T(8,128)} %copy.14, f32[1024]{0:T(1024)S(1)} %div.37, bf16[1024,1152]{1,0:T(8,128)(2,1)S(1)} %copy-done, f32[1024]{0:T(1024)S(1)} %add_rsqrt_fusion, f32[1024]{0:T(1024)S(1)} %broadcast_multiply_fusion), kind=kOutput, calls=%fused_computation.14 | convolution fusion | flops 5125996544 | bytes 29917184 | tf_op jit(solution)/shard_map/dot_general | solution.py:95
  107.7 0.0 reduce-scatter.4.cloned.1.call-update
  107.8 0.5 broadcast_multiply_fusion.1
  108.3 19.2 %all_gather.13 = bf16[256,1152]{1,0:T(8,128)(2,1)S(1)} all-gather(bf16[16,1152]{1,0:T(8,128)(2,1)S(1)} %multiply_convert_fusion.2), channel_id=1, replica_groups=mesh['dp'=16,'mp'=2] {'dp'}, dimensions={0}, use_global_device_ids=true | all-gather | bytes 626688 | tf_op jit(solution)/shard_map/all_gather | solution.py:103
  127.5 0.7 fusion.22
  128.2 22.1 %all_gather.14 = bf16[256,1152]{1,0:T(8,128)(2,1)S(1)} all-gather(bf16[16,1152]{1,0:T(8,128)(2,1)S(1)} %multiply_convert_fusion.1), channel_id=1, replica_groups=mesh['dp'=16,'mp'=2] {'dp'}, dimensions={0}, use_global_device_ids=true | all-gather | bytes 626688 | tf_op jit(solution)/shard_map/all_gather | solution.py:111
  150.3 0.7 fusion.24
  151.0 0.0 all-gather.2.cloned.1.call-done
  151.0 2.5 %fusion.26 = f32[72,2152]{1,0:T(8,128)} fusion(bf16[256,2152]{1,0:T(8,128)(2,1)} %all-gather.2.cloned.1.call-done, bf16[256,1152]{1,0:T(8,128)(2,1)S(1)} %all_gather.14, s32[]{:T(128)S(6)} %select_n.23), kind=kOutput, calls=%fused_computation.40 | convolution fusion | flops 79331328 | bytes 1787140 | tf_op jit(solution)/shard_map/dot_general | solution.py:113
  153.5 68.5 %reduce-scatter.4.cloned.1.call-done = f32[72,2152]{1,0:T(8,128)} async-done(((f32[1152,2152]{1,0:T(8,128)}), f32[72,2152]{1,0:T(8,128)}) %reduce-scatter.4.cloned.1.call-update) | async-done | bytes 619792
  (4 shorter events, 0.0 us)
Async XLA Ops:
  8.0 64.8 %all-reduce.3.cloned.1.call-start = ((), (), s32[]{:S(2)}) async-start(), calls=%async_computation.1 | async-start | bytes 147456 | tf_op jit(solution)/shard_map/psum | solution.py:80
  27.4 9.2 %copy-start.4 = (s32[16]{0:T(128)S(1)}, s32[16]{0:T(128)}, u32[]{:S(2)}) copy-start(s32[16]{0:T(128)} %param.7) | copy-start | bytes 196
  36.6 9.6 %copy-start = (bf16[1024,1152]{1,0:T(8,128)(2,1)S(1)}, bf16[1024,1152]{1,0:T(8,128)(2,1)}, u32[]{:S(2)}) copy-start(bf16[1024,1152]{1,0:T(8,128)(2,1)} %param.6) | copy-start | bytes 7077892
  36.6 10.7 %copy-start.2 = (bf16[16,1152]{1,0:T(8,128)(2,1)S(1)}, bf16[16,1152]{1,0:T(8,128)(2,1)}, u32[]{:S(2)}) copy-start(bf16[16,1152]{1,0:T(8,128)(2,1)} %param.8) | copy-start | bytes 110596
  36.6 36.1 %copy-start.3 = (s32[256]{0:T(256)S(1)}, s32[256]{0:T(256)}, u32[]{:S(2)}) copy-start(s32[256]{0:T(256)} %param.9) | copy-start | bytes 3076
  41.8 3.9 %copy-start.1 = (bf16[16,2152]{1,0:T(8,128)(2,1)}, bf16[16,2152]{1,0:T(8,128)(2,1)S(1)}, u32[]{:S(2)}) copy-start(bf16[16,2152]{1,0:T(8,128)(2,1)S(1)} %multiply_reduce_fusion) | copy-start | bytes 206596
  45.6 105.3 %all-gather.2.cloned.1.call-start = ((), (), s32[]{:S(2)}) async-start(), calls=%async_computation.2 | async-start | bytes 1183744 | tf_op jit(solution)/shard_map/all_gather | solution.py:110
  46.2 175.8 %reduce-scatter.4.cloned.1.call-start = ((), (), s32[]{:S(2)}) async-start(), calls=%async_computation.3 | async-start | bytes 10653696
Sparse Core Ops, SparseCore 0:
  45.8 23.4 all-reduce.2
Sparse Core Ops, SparseCore 1:
  49.0 41.2 all-gather.1
  107.8 114.1 reduce-scatter.3

commit v2 on v1

--- a/solution.py
+++ b/solution.py
@@ -1,6 +1,8 @@
 import jax
 import jax.numpy as jnp
 from jax import lax
+from jax.experimental import pallas as pl
+from jax.experimental.pallas import tpu as pltpu
 from jax.sharding import PartitionSpec as P
 
 LOGIT_SCALE = 117.0
@@ -27,6 +29,201 @@
 def unit_rows(rows):
     scale = lax.rsqrt(jnp.sum(rows * rows, 1, keepdims=True) + 1e-06)
     return (rows * scale, scale)
+
+
+LANES = 128
+SLABS = 3
+MESH = pl.DeviceIdType.MESH
+
+
+def slab_width(hidden):
+    return -(-hidden // (2 * SLABS * LANES)) * LANES
+
+
+def sum_over_chips_kernel(
+    own_ref, other_ref, grad_ref, out_ref, grad_other, keep, x_out, x_in, near_out, near_in,
+    far_out, far_in, swap_out, swap_in, grad_sems, x_sems, near_sems, far_sems, swap_sems
+):
+    rank = lax.axis_index("dp")
+    column = lax.axis_index("mp")
+    core = rank % 2
+    x = (rank // 2) % 2
+    z = rank // 4
+    low, high = z % 2, z // 2
+    width = grad_other.shape[2]
+    half = SLABS * width
+    rows = keep.shape[2]
+    own_rows = rows // 2
+
+    def device(z_at, x_at, core_at):
+        return ((z_at * 2 + x_at) * 2 + core_at, column)
+
+    core_peer = device(z, x, 1 - core)
+    x_peer = device(z, 1 - x, core)
+    near_peer = device(z + 1 - 2 * low, x, core)
+    far_peer = device(z + 2 - 4 * high, x, core)
+
+    barrier = pltpu.get_barrier_semaphore()
+    for peer in (core_peer, x_peer, near_peer, far_peer):
+        pl.semaphore_signal(barrier, inc=1, device_id=peer, device_id_type=MESH)
+    pl.semaphore_wait(barrier, 4)
+
+    def copy(src, dst, sems, index, peer):
+        return pltpu.make_async_remote_copy(
+            src_ref=src,
+            dst_ref=dst,
+            send_sem=sems.at[0, index],
+            recv_sem=sems.at[1, index],
+            device_id=peer,
+            device_id_type=MESH,
+        )
+
+    def columns(which, slab):
+        return pl.ds(pl.multiple_of(which * half + slab * width, LANES), width)
+
+    def grad_copy(slab):
+        return copy(
+            grad_ref.at[:, columns(1 - core, slab)], grad_other.at[slab], grad_sems, slab, core_peer
+        )
+
+    def x_copy(step):
+        return copy(x_out.at[step], x_in.at[step], x_sems, step, x_peer)
+
+    def near_copy(step):
+        return copy(near_out.at[step], near_in.at[step], near_sems, step, near_peer)
+
+    def far_copy(step):
+        return copy(far_out.at[step], far_in.at[step], far_sems, step, far_peer)
+
+    def swap_copy(step):
+        return copy(swap_out.at[step], swap_in.at[step], swap_sems, step, core_peer)
+
+    for slab in range(SLABS):
+        grad_copy(slab).start()
+
+    def block(d0, d1, x_at, slab):
+        z_at = z + d0 * (1 - 2 * low) + d1 * (2 - 4 * high)
+        at = pl.ds(pl.multiple_of((z_at * 2 + x_at) * rows, 16), rows)
+        return jnp.dot(
+            own_ref[at, :], grad_ref[:, columns(core, slab)], preferred_element_type=jnp.float32
+        ) + jnp.dot(other_ref[at, :], grad_other[slab], preferred_element_type=jnp.float32)
+
+    for slab in range(SLABS):
+        grad_copy(slab).wait_recv()
+
+        @pl.loop(0, 1)
+        def _(unused, slab=slab):
+            x_out[slab] = block(1, 1, 1 - x, slab).astype(jnp.bfloat16)
+            x_copy(slab).start()
+
+    @pl.loop(SLABS, 4 * SLABS)
+    def _(step):
+        turn, slab = step // SLABS, step % SLABS
+        x_out[step] = block(1 - turn % 2, 1 - turn // 2, 1 - x, slab).astype(jnp.bfloat16)
+        x_copy(step).start()
+
+    @pl.loop(0, 4 * SLABS)
+    def _(step):
+        turn, slab = step // SLABS, step % SLABS
+        keep[step // SLABS, step % SLABS] = block(1 - turn % 2, 1 - turn // 2, x, slab)
+
+    @pl.loop(0, SLABS)
+    def _(slab):
+        x_copy(slab).wait_recv()
+        near_out[slab] = (keep[0, slab] + x_in[slab].astype(jnp.float32)).astype(jnp.bfloat16)
+        near_copy(slab).start()
+
+    @pl.loop(0, SLABS)
+    def _(slab):
+        x_copy(SLABS + slab).wait_recv()
+        near_copy(slab).wait_recv()
+        far_out[slab] = (
+            keep[1, slab]
+            + x_in[SLABS + slab].astype(jnp.float32)
+            + near_in[slab].astype(jnp.float32)
+        ).astype(jnp.bfloat16)
+        far_copy(slab).start()
+
+    @pl.loop(0, SLABS)
+    def _(slab):
+        x_copy(2 * SLABS + slab).wait_recv()
+        near_out[SLABS + slab] = (
+            keep[2, slab] + x_in[2 * SLABS + slab].astype(jnp.float32)
+        ).astype(jnp.bfloat16)
+        near_copy(SLABS + slab).start()
+
+    for slab in range(SLABS):
+        x_copy(3 * SLABS + slab).wait_recv()
+        near_copy(SLABS + slab).wait_recv()
+        far_copy(slab).wait_recv()
+        keep[3, slab] = (
+            keep[3, slab]
+            + x_in[3 * SLABS + slab].astype(jnp.float32)
+            + near_in[SLABS + slab].astype(jnp.float32)
+            + far_in[slab].astype(jnp.float32)
+        )
+        theirs = pl.ds(pl.multiple_of((1 - core) * own_rows, 8), own_rows)
+        mine = pl.ds(pl.multiple_of(core * own_rows, 8), own_rows)
+        swap_out[slab] = keep[3, slab, theirs, :]
+        swap_copy(slab).start()
+        out_ref[:, columns(core, slab)] = keep[3, slab, mine, :]
+
+    for slab in range(SLABS):
+        swap_copy(slab).wait_recv()
+        out_ref[:, columns(1 - core, slab)] = swap_in[slab]
+
+    for slab in range(SLABS):
+        grad_copy(slab).wait_send()
+        far_copy(slab).wait_send()
+        swap_copy(slab).wait_send()
+
+    @pl.loop(0, 4 * SLABS)
+    def _(step):
+        x_copy(step).wait_send()
+
+    @pl.loop(0, 2 * SLABS)
+    def _(step):
+        near_copy(step).wait_send()
+
+
+def sum_over_chips(own_t, other_t, pre_grad):
+    features, tokens = own_t.shape
+    width = pre_grad.shape[1] // (2 * SLABS)
+    rows = features // 8
+    own_rows = rows // 2
+    bf16, f32 = jnp.bfloat16, jnp.float32
+    vmem = pl.BlockSpec(memory_space=pltpu.VMEM)
+    dma = pltpu.SemaphoreType.DMA
+    flops = 4 * features * tokens * pre_grad.shape[1] // 2
+    return pl.pallas_call(
+        sum_over_chips_kernel,
+        out_shape=jax.ShapeDtypeStruct((own_rows, pre_grad.shape[1]), f32),
+        in_specs=[vmem] * 3,
+        out_specs=vmem,
+        scratch_shapes=[
+            pltpu.VMEM((SLABS, tokens, width), bf16),
+            pltpu.VMEM((4, SLABS, rows, width), f32),
+            pltpu.VMEM((4 * SLABS, rows, width), bf16),
+            pltpu.VMEM((4 * SLABS, rows, width), bf16),
+            pltpu.VMEM((2 * SLABS, rows, width), bf16),
+            pltpu.VMEM((2 * SLABS, rows, width), bf16),
+            pltpu.VMEM((SLABS, rows, width), bf16),
+            pltpu.VMEM((SLABS, rows, width), bf16),
+            pltpu.VMEM((SLABS, own_rows, width), f32),
+            pltpu.VMEM((SLABS, own_rows, width), f32),
+            dma((2, SLABS)),
+            dma((2, 4 * SLABS)),
+            dma((2, 2 * SLABS)),
+            dma((2, SLABS)),
+            dma((2, SLABS)),
+        ],
+        cost_estimate=pl.CostEstimate(
+            flops=flops, bytes_accessed=4 * features * pre_grad.shape[1], transcendentals=0
+        ),
+        compiler_params=pltpu.CompilerParams(
+            collective_id=0, has_side_effects=True, vmem_limit_bytes=48 * 1024 * 1024
+        ),
+    )(own_t, other_t, pre_grad)
 
 
 def signed_logits(text_rows, text_group, image_rows, image_group):
@@ -62,7 +259,8 @@
 
     unit_image, image_scale = unit_rows(images.astype(jnp.float32))
     image_half = unit_image.astype(jnp.bfloat16)
-    all_images = lax.all_gather(image_half, "dp", axis=0, tiled=True)
+    all_images = lax.all_gather(unit_image, "dp", axis=0, tiled=True)
+    all_images = lax.optimization_barrier(all_images).astype(jnp.bfloat16)
 
     tok_float = tokens.astype(jnp.float32)
     normed = layer_norm(tok_float).astype(jnp.bfloat16)
@@ -86,29 +284,43 @@
     text_back = jnp.dot(loss_slope(signs, signed), all_images, preferred_element_type=jnp.float32)
     pooled_half = through_unit(text_back, unit_text, text_scale).astype(jnp.bfloat16)
 
+    gathered = lax.all_gather(
+        jnp.concatenate([text_half, pooled_half, gbar], 1), "dp", axis=0, tiled=True
+    )
+    all_texts = gathered[:, :width]
+    all_pooled = gathered[:, width : 2 * width]
+    all_gbar = gathered[:, 2 * width :]
+
+    by_chips = devices == 16 and width % 128 == 0
+    if by_chips:
+        padding = 2 * SLABS * slab_width(hidden) - hidden
+        w_down = jnp.pad(w_down, ((0, 0), (0, padding)))
+        slope = jnp.pad(slope, ((0, 0), (0, padding)))
     hidden_grad = jnp.dot(pooled_half, w_down, preferred_element_type=jnp.float32)
     pre_grad = (
-        share[:, :, None] * hidden_grad[:, None, :] * slope.reshape(captions, seq_len, hidden)
+        share[:, :, None] * hidden_grad[:, None, :] * slope.reshape(captions, seq_len, -1)
     ).astype(jnp.bfloat16)
-    pre_grad = pre_grad.reshape(captions * seq_len, hidden)
-    up_grad = lax.psum_scatter(
-        lax.dot_general(
-            normed, pre_grad, (((0,), (0,)), ((), ())), preferred_element_type=jnp.float32
-        ),
-        "dp",
-        scatter_dimension=0,
-        tiled=True,
-    )
-
-    all_texts = lax.all_gather(text_half, "dp", axis=0, tiled=True)
+    pre_grad = pre_grad.reshape(captions * seq_len, -1)
+    if by_chips:
+        normed_t = normed.T
+        other_t = lax.ppermute(normed_t, "dp", [(i, i ^ 1) for i in range(devices)])
+        up_grad = sum_over_chips(normed_t, other_t, pre_grad)[:, :hidden]
+    else:
+        up_grad = lax.psum_scatter(
+            lax.dot_general(
+                normed, pre_grad, (((0,), (0,)), ((), ())), preferred_element_type=jnp.float32
+            ),
+            "dp",
+            scatter_dimension=0,
+            tiled=True,
+        )
+
     signs, signed = signed_logits(all_texts, pair_group, image_half, own_group)
     image_back = lax.dot_general(
         loss_slope(signs, signed), all_texts, (((0,), (0,)), ((), ())),
         preferred_element_type=jnp.float32,
     )
     image_grad = through_unit(image_back, unit_image, image_scale)
-    all_gbar = lax.all_gather(gbar, "dp", axis=0, tiled=True)
-    all_pooled = lax.all_gather(pooled_half, "dp", axis=0, tiled=True)
     own_pooled = lax.dynamic_slice_in_dim(all_pooled, own_index * own_rows, own_rows, 1)
     down_grad = lax.dot_general(
         own_pooled, all_gbar, (((0,), (0,)), ((), ())), preferred_element_type=jnp.float32

time: 230 us -> 142 us (0.62)
  waiting for transfers between devices: 69.1 us -> 0.04 us
  Pallas kernels: 0 us -> 49.5 us
  blocking collectives: 66.5 us -> 25 us
  matrix products: 42.1 us -> 23 us
  local copies, waits for them, and re-layouts: 22.9 us -> 8.11 us
  other arithmetic: 13.2 us -> 20.3 us
    unnamed x4 -> x2, waiting for transfers between devices: 69.1 us -> 0.03 us
    pallas_call x0 -> x1, Pallas kernels: none -> 49.5 us  [sum_over_chips(): pl.pallas_call(sum_over_chips_kernel, out_shape=jax.ShapeDtypeStruct((own...]
    all_gather x3 -> x1, blocking collectives: 66.5 us -> 25 us  [on_device(): all_images = lax.all_gather(unit_image, 'dp', axis=0, tiled=True)]
    mul x3 -> x0, local copies, waits for them, and re-layouts: 22.8 us -> none  [the longest x2 13.5 us: on_device(): share[:, :, None] * hidden_grad[:, None, :]]
    dot_general x1 -> x0, matrix products: 15.5 us -> none  [on_device(): lax.dot_general(normed, pre_grad, (((0,), (0,)), ((), ())), preferred_ele...]
    add x0 -> x1, other arithmetic: none -> 7.26 us  [gelu_pair(): 0.5 * (1.0 + tanh_u)]
    reduce_sum x1 -> x0, other arithmetic: 4.85 us -> none  [on_device(): jnp.sum(value.reshape(captions, seq_len, hidden) * share[:, :, None], 1)]
    convert_element_type x0 -> x1, local copies, waits for them, and re-layouts: none -> 3.12 us  [on_device(): tok_float = tokens.astype(jnp.float32)]
  transfers between devices with their start and end apart: 3 -> 3, of which waited for: 1 -> 0; matrix products, arithmetic and copies ran while one was open for 18% -> 17% of each run, Pallas kernels for 0% -> 35%
where the time goes in v2:
time: 142 us; the launch traced here: 141 us
  Pallas kernels  49.5 us (35%)
  blocking collectives  25 us (18%)
  matrix products  23 us (16%)
  other arithmetic  20.3 us (14%)
  between operations  14.2 us (10%)
  local copies, waits for them, and re-layouts  8.11 us (6%)
    pallas_call x1, Pallas kernels, sum_over_chips(): pl.pallas_call(sum_over_chips_kernel, out_shape=jax.ShapeDtypeStruct((own...  49.5 us
    all_gather x1, blocking collectives, on_device(): all_images = lax.all_gather(unit_image, 'dp', axis=0, tiled=True)  25 us
    dot_general x1, matrix products, on_device(): pre = jnp.dot(normed, w_up, preferred_element_type=jnp.float32)  12.5 us
    add x1, other arithmetic, gelu_pair(): 0.5 * (1.0 + tanh_u)  7.26 us
    dot_general x1, matrix products, on_device(): jnp.dot(pooled_half, w_down, preferred_element_type=jnp.float32)  3.81 us
    convert_element_type x1, local copies, waits for them, and re-layouts, on_device(): tok_float = tokens.astype(jnp.float32)  3.12 us
    convert_element_type x1, other arithmetic, on_device(): pre_grad = (share[:, :, None] * hidden_grad[:, None, :] * slope.reshape(c...  3.01 us
    reduce_sum x1, other arithmetic, on_device(): jnp.sum(tok_float.reshape(captions, seq_len, width) * share[:, :, None], 1)  3 us
  transfers between devices with their start and end apart: 3, of which 0 were waited for; matrix products, arithmetic and copies ran while one was open for 17% of the time, Pallas kernels for 35%

profile of v2, /device:TPU:0, one launch (start us, length us, event | category | flops | bytes accessed | tf_op | source)
XLA Modules:
  0.0 140.5 jit_solution(5781394452439947074)
XLA Ops:
  7.2 0.0 copy-start.3
  7.2 0.0 all-reduce.4.cloned.1.call-start
  7.2 2.8 %copy.27 = bf16[1024,1152]{0,1:T(8,128)(2,1)S(1)} copy(bf16[1024,1152]{1,0:T(8,128)(2,1)} %param.6) | data formatting | bytes 4718592 | tf_op args[0]
  10.1 0.0 copy-start
  10.1 0.4 convert_reduce_fusion
  10.5 0.0 slice-start
  10.5 0.7 multiply_reduce_fusion.1
  11.2 0.0 copy-done.3
  11.2 0.2 convert_reduce_fusion.1
  11.4 0.1 convert_divide_fusion
  11.5 12.5 %multiply_reduce_fusion = (bf16[16,2152]{1,0:T(8,128)(2,1)S(1)}, f32[1024,2152]{1,0:T(8,128)}) fusion(f32[16,64]{1,0:T(8,128)S(1)} %convert_divide_fusion, bf16[1152,2152]{0,1:T(8,128)(2,1)} %param.10, bf16[1024,1152]{0,1:T(8,128)(2,1)S(1)} %copy.27, f32[1024]{0:T(1024)S(1)} %add_rsqrt_fusion, f32[1024]{0:T(1024)S(1)} %broadcast_multiply_fusion), kind=kOutput, calls=%fused_computation.10 | convolution fusion | flops 5103925760 | bytes 16213248 | tf_op jit(solution)/shard_map/dot_general | solution.py:267
  24.0 0.0 slice-done
  24.0 0.0 slice-done.1
  24.0 1.4 %fusion.67 = f32[16,1152]{1,0:T(8,128)} fusion(bf16[16,2152]{1,0:T(8,128)(2,1)S(1)} %get-tuple-element.6, bf16[1152,2152]{0,1:T(8,128)(2,1)S(1)} %bitcast.20), kind=kOutput, calls=%fused_computation.89 | convolution fusion | flops 79331328 | bytes 5100800 | tf_op jit(solution)/shard_map/dot_general | solution.py:275
  25.4 0.0 all-reduce.4.cloned.1.call-update
  25.5 0.0 copy-start.1
  25.5 0.0 copy-start.2
  25.5 0.0 all-gather.2.cloned.1.call-start
  25.5 0.0 copy-done
  25.5 3.1 %copy.28 = f32[1024,1152]{1,0:T(8,128)} copy(bf16[1024,1152]{0,1:T(8,128)(2,1)S(1)} %copy.27) | data formatting | bytes 7077888 | tf_op jit(solution)/shard_map/convert_element_type | solution.py:265
  28.7 3.0 %multiply_reduce_fusion.2 = f32[16,1152]{1,0:T(8,128)S(1)} fusion(f32[16,64]{1,0:T(8,128)S(1)} %convert_divide_fusion, f32[1024,1152]{1,0:T(8,128)} %copy.28), kind=kLoop, calls=%fused_computation.16 | loop fusion | flops 2340864 | bytes 4796416 | tf_op jit(solution)/shard_map/reduce_sum | solution.py:273
  31.7 0.0 copy-done.1
  31.7 0.1 fusion.28
  31.8 0.1 convert_multiply_fusion
  31.9 25.0 %all_gather.6 = bf16[256,1152]{1,0:T(8,128)(2,1)S(1)} all-gather(bf16[16,1152]{1,0:T(8,128)(2,1)S(1)} %convert_multiply_fusion), channel_id=1, replica_groups=mesh['dp'=16,'mp'=2] {'dp'}, dimensions={0}, use_global_device_ids=true | all-gather | bytes 626688 | tf_op jit(solution)/shard_map/all_gather | solution.py:262
  56.9 0.0 copy-done.2
  56.9 0.1 dynamic_slice.6
  57.0 1.0 multiply_reduce_fusion.5
  58.0 0.1 multiply_convert_fusion.3
  58.1 0.4 fusion.39
  58.5 0.4 multiply_reduce_fusion.4
  58.8 0.1 multiply_convert_fusion.2
  58.9 0.7 pad_maximum_fusion
  59.6 0.0 all-gather.2.cloned.1.call-update
  59.6 2.3 %fusion.9.own_ref = bf16[1152,1024]{1,0:T(8,128)(2,1)S(1)} fusion(f32[1024]{0:T(1024)S(1)} %add_rsqrt_fusion, f32[1024]{0:T(1024)S(1)} %broadcast_multiply_fusion, bf16[1024,1152]{0,1:T(8,128)(2,1)} %copy-done), kind=kLoop, calls=%fused_computation.18 | loop fusion | flops 4718592 | bytes 4726784 | tf_op jit(solution)/shard_map/transpose | solution.py:305
  62.0 0.4 collective-permute-start
  62.4 0.1 div.38
  62.5 7.3 %fusion.6 = f32[1024,2152]{1,0:T(8,128)S(1)} fusion(f32[1024,2152]{1,0:T(8,128)} %get-tuple-element.7), kind=kLoop, calls=%fused_computation.9 | loop fusion | flops 37462016 | bytes 17629184 | tf_op jit(solution)/shard_map/add | solution.py:23
  69.7 3.8 %fusion.7 = f32[16,2304]{1,0:T(8,128)S(1)} fusion(bf16[16,1152]{1,0:T(8,128)(2,1)S(1)} %multiply_convert_fusion.2, bf16[1152,2152]{0,1:T(8,128)(2,1)} %param.11), kind=kOutput, calls=%fused_computation.12 | convolution fusion | flops 84934656 | bytes 5142528 | tf_op jit(solution)/shard_map/dot_general | solution.py:299
  73.5 3.0 %fusion.1.grad_ref = bf16[1024,2304]{1,0:T(8,128)(2,1)} fusion(f32[1024,2152]{1,0:T(8,128)S(1)} %fusion.6, f32[16,2304]{1,0:T(8,128)S(1)} %fusion.7, f32[1024]{0:T(1024)S(1)} %div.38), kind=kLoop, calls=%fused_computation.4 | loop fusion | flops 7077888 | bytes 13684736 | tf_op jit(solution)/shard_map/convert_element_type | solution.py:302
  76.6 0.5 broadcast_multiply_fusion.1
  77.1 0.0 collective-permute-done.other_ref
  77.1 49.5 %shard_map.93 = f32[72,2304]{1,0:T(8,128)S(1)} custom-call(bf16[1152,1024]{1,0:T(8,128)(2,1)S(1)} %fusion.9.own_ref, bf16[1152,1024]{1,0:T(8,128)(2,1)} %collective-permute-done.other_ref, bf16[1024,2304]{1,0:T(8,128)(2,1)} %fusion.1.grad_ref), custom_call_target="tpu_custom_call" | custom-call | flops 5435817984 | bytes 10616832 | tf_op jit(solution)/shard_map/pallas_call | solution.py:198
  126.5 0.9 slice.13
  127.4 2.0 %multiply_reduce_fusion.3 = (f32[16]{0:T(128)S(1)}, f32[16,1152]{1,0:T(8,128)S(1)}) fusion(bf16[16,1152]{1,0:T(8,128)(2,1)S(1)} %copy-done.1, f32[16]{0:T(128)S(1)} %add_rsqrt_fusion.1, bf16[256,4456]{1,0:T(8,128)(2,1)} %all-gather.2.cloned.1.call-done, s32[256]{0:T(256)S(1)} %copy-done.2, s32[16]{0:T(128)S(1)} %dynamic_slice.6), kind=kOutput, calls=%fused_computation.43 | convolution fusion | flops 19044336 | bytes 1329728 | tf_op jit(solution)/shard_map/dot_general | solution.py:319
  129.4 0.7 subtract_multiply_fusion
  130.1 1.1 slice.17
  131.2 2.5 %fusion.11 = f32[72,2152]{1,0:T(8,128)} fusion(bf16[256,4456]{1,0:T(8,128)(2,1)} %all-gather.2.cloned.1.call-done, bf16[256,1152]{1,0:T(8,128)(2,1)S(1)} %slice.17, s32[]{:T(128)S(6)} %select_n.23), kind=kOutput, calls=%fused_computation.20 | convolution fusion | flops 79331328 | bytes 1799428 | tf_op jit(solution)/shard_map/dot_general | solution.py:325
  (8 shorter events, 0.0 us)
Async XLA Ops:
  7.2 4.0 %copy-start.3 = (s32[16]{0:T(128)S(1)}, s32[16]{0:T(128)}, u32[]{:S(2)}) copy-start(s32[16]{0:T(128)} %param.7) | copy-start | bytes 196
  7.2 49.8 %all-reduce.4.cloned.1.call-start = ((), (), s32[]{:S(2)}) async-start(), calls=%async_computation | async-start | bytes 147456 | tf_op jit(solution)/shard_map/psum | solution.py:278
  10.1 15.5 %copy-start = (bf16[1024,1152]{0,1:T(8,128)(2,1)}, bf16[1024,1152]{0,1:T(8,128)(2,1)S(1)}, u32[]{:S(2)}) copy-start(bf16[1024,1152]{0,1:T(8,128)(2,1)S(1)} %copy.27) | copy-start | bytes 7077892
  10.5 13.5 %slice-start = ((s8[4958208]{0:T(1024)(128)(4,1)}), s8[4194304]{0:T(1024)(128)(4,1)S(1)}, s32[]{:S(2)}) async-start(s8[4958208]{0:T(1024)(128)(4,1)} %bitcast.19), calls=%async_computation.2 | async-start | bytes 8388608
  11.4 12.6 %slice-start.1 = ((s8[4958208]{0:T(1024)(128)(4,1)}), s8[763904]{0:T(1024)(128)(4,1)S(1)}, s32[]{:S(2)}) async-start(s8[4958208]{0:T(1024)(128)(4,1)} %bitcast.19), calls=%async_computation.3 | async-start | bytes 1527808
  25.5 6.2 %copy-start.1 = (bf16[16,1152]{1,0:T(8,128)(2,1)S(1)}, bf16[16,1152]{1,0:T(8,128)(2,1)}, u32[]{:S(2)}) copy-start(bf16[16,1152]{1,0:T(8,128)(2,1)} %param.8) | copy-start | bytes 110596
  25.5 31.4 %copy-start.2 = (s32[256]{0:T(256)S(1)}, s32[256]{0:T(256)}, u32[]{:S(2)}) copy-start(s32[256]{0:T(256)} %param.9) | copy-start | bytes 3076
  25.5 101.9 %all-gather.2.cloned.1.call-start = ((), (), s32[]{:S(2)}) async-start(), calls=%async_computation.1 | async-start | bytes 2437120 | tf_op jit(solution)/shard_map/all_gather | solution.py:287
  62.0 15.1 %collective-permute-start = (bf16[1152,1024]{1,0:T(8,128)(2,1)S(1)}, bf16[1152,1024]{1,0:T(8,128)(2,1)}, u32[]{:S(2)}, u32[]{:S(2)}) collective-permute-start(bf16[1152,1024]{1,0:T(8,128)(2,1)S(1)} %fusion.9.own_ref), channel_id=1, source_target_pairs={{0,2},{2,0},{4,6},{6,4},{8,10},{10,8},{12,14},{14,12},{16,18},{18,... | collective-permute-start | bytes 7077896 | tf_op jit(solution)/shard_map/ppermute | solution.py:306
Sparse Core Ops, SparseCore 0:
  25.6 23.3 all-reduce.3
  59.8 50.7 all-gather.1

commit v3 on v2

--- a/solution.py
+++ b/solution.py
@@ -1,3 +1,5 @@
+import functools
+
 import jax
 import jax.numpy as jnp
 from jax import lax
@@ -17,12 +19,10 @@
 
 def gelu_pair(pre):
     const = 0.7978845608028654
-    inner = const * (pre + 0.044715 * pre * pre * pre)
-    tanh_u = jnp.tanh(inner)
-    value = 0.5 * pre * (1.0 + tanh_u)
-    slope = 0.5 * (1.0 + tanh_u) + 0.5 * pre * (1.0 - tanh_u * tanh_u) * const * (
-        1.0 + 3.0 * 0.044715 * pre * pre
-    )
+    square = pre * pre
+    half = 0.5 + 0.5 * jnp.tanh(pre * (const + const * 0.044715 * square))
+    value = pre * half
+    slope = half + value * (1.0 - half) * (2.0 * const + 6.0 * const * 0.044715 * square)
     return (value, slope)
 
 
@@ -31,6 +31,26 @@
     return (rows * scale, scale)
 
 
+def signed_logits(text_rows, text_group, image_rows, image_group):
+    logits = (
+        LOGIT_SCALE
+        * lax.dot_general(
+            text_rows, image_rows, (((1,), (1,)), ((), ())), preferred_element_type=jnp.float32
+        )
+        + LOGIT_SHIFT
+    )
+    signs = jnp.where(text_group == image_group, 1.0, -1.0).astype(jnp.float32)
+    return (signs, signs * logits)
+
+
+def loss_slope(signs, signed):
+    return (-LOGIT_SCALE * signs * jax.nn.sigmoid(-signed)).astype(jnp.bfloat16)
+
+
+def through_unit(back, unit, scale):
+    return (back - unit * jnp.sum(unit * back, 1, keepdims=True)) * scale
+
+
 LANES = 128
 SLABS = 3
 MESH = pl.DeviceIdType.MESH
@@ -40,8 +60,257 @@
     return -(-hidden // (2 * SLABS * LANES)) * LANES
 
 
+class Place:
+    def __init__(self):
+        rank = lax.axis_index("dp")
+        self.column = lax.axis_index("mp")
+        self.rank = rank
+        self.core = rank % 2
+        self.x = (rank // 2) % 2
+        self.z = rank // 4
+        self.low, self.high = self.z % 2, self.z // 2
+
+    def toward(self, far, near, across, other):
+        z = self.z + far * (2 - 4 * self.high) + near * (1 - 2 * self.low)
+        x = self.x + across * (1 - 2 * self.x)
+        core = self.core + other * (1 - 2 * self.core)
+        return (z * 2 + x) * 2 + core
+
+    def peer(self, *flips):
+        return (self.toward(*flips), self.column)
+
+    def mp_peer(self):
+        return (self.rank, 1 - self.column)
+
+
+def meet(peers):
+    barrier = pltpu.get_barrier_semaphore()
+    for peer in peers:
+        pl.semaphore_signal(barrier, inc=1, device_id=peer, device_id_type=MESH)
+    pl.semaphore_wait(barrier, len(peers))
+
+
+def remote(src, dst, sems, index, peer):
+    return pltpu.make_async_remote_copy(
+        src_ref=src,
+        dst_ref=dst,
+        send_sem=sems.at[0, index],
+        recv_sem=sems.at[1, index],
+        device_id=peer,
+        device_id_type=MESH,
+    )
+
+
+def forward_kernel(
+    total, tok_ref, share_ref, img_ref, group_ref, own_group_ref, up_hbm, down_hbm,
+    gbar_ref, text_ref, pooled_ref, loss_ref, hidden_ref, slope_ref, own_t, other_t,
+    w_up, w_down, normed, pre_a, pre_b, gmean, tmean, images, mine, theirs,
+    local_sems, img_sems, mp_sems, t_sems
+):
+    place = Place()
+    captions = gbar_ref.shape[0]
+    hidden = gbar_ref.shape[1]
+    tokens = tok_ref.shape[0]
+    seq_len = tokens // captions
+    width = slab_width(hidden)
+    tile = tokens // 2
+    tile_captions = captions // 2
+    last = hidden // width * width
+    f32, bf16 = jnp.float32, jnp.bfloat16
+
+    up_copy = pltpu.make_async_copy(up_hbm, w_up, local_sems.at[0])
+    down_copy = pltpu.make_async_copy(down_hbm, w_down, local_sems.at[1])
+    up_copy.start()
+    down_copy.start()
+
+    unit, unused = unit_rows(img_ref[...].astype(f32))
+
+    def block_of(rank):
+        return pl.ds(pl.multiple_of(rank * captions, 16), captions)
+
+    images[block_of(place.rank), :] = unit.astype(bf16)
+    far, near, across, core = (1, 0, 0, 0), (0, 1, 0, 0), (0, 0, 1, 0), (0, 0, 0, 1)
+    meet([place.peer(*far), place.peer(*near), place.peer(*across), place.peer(*core),
+          place.mp_peer()])
+
+    stages = (far, near, across, core)
+
+    def img_copies(stage):
+        copies = []
+        for held in range(1 << stage):
+            flips = [(held >> bit) & 1 if bit < stage else 0 for bit in range(4)]
+            at = block_of(place.toward(*flips))
+            copies.append(
+                remote(images.at[at, :], images.at[at, :], img_sems, (1 << stage) - 1 + held,
+                       place.peer(*stages[stage]))
+            )
+        return copies
+
+    def img_start(stage):
+        for c in img_copies(stage):
+            c.start()
+
+    def img_wait(stage):
+        for c in img_copies(stage):
+            c.wait_recv()
+
+    img_start(0)
+
+    @pl.loop(0, 2)
+    def _(turn):
+        at = pl.ds(pl.multiple_of(turn * tile, 16), tile)
+        tok = tok_ref[at, :].astype(f32)
+        normed[at, :] = layer_norm(tok).astype(bf16)
+        shared = (tok * share_ref[at, 0:1]).reshape(tile_captions, seq_len, tok.shape[1])
+        tmean[pl.ds(pl.multiple_of(turn * tile_captions, 8), tile_captions), :] = jnp.sum(
+            shared, 1
+        )
+
+    img_wait(0)
+    img_start(1)
+    up_copy.wait()
+
+    def project(dst, turn, cols, size):
+        dst[:, :size] = jnp.dot(
+            normed[turn * tile : (turn + 1) * tile, :], w_up[:, cols], preferred_element_type=f32
+        )
+
+    def activate(src, turn, cols, size):
+        rows = slice(turn * tile, (turn + 1) * tile)
+        value, slope = gelu_pair(src[:, :size])
+        slope_ref[rows, cols] = slope
+        shared = (value * share_ref[rows, 0:1]).reshape(tile_captions, seq_len, size)
+        gmean[turn * tile_captions : (turn + 1) * tile_captions, cols] = jnp.sum(shared, 1)
+
+    def slab_columns(slab):
+        return pl.ds(pl.multiple_of(slab * width, LANES), width)
+
+    project(pre_a, 0, slice(0, width), width)
+
+    @pl.loop(0, last // width - 1)
+    def _(slab):
+        project(pre_b, 1, slab_columns(slab), width)
+        activate(pre_a, 0, slab_columns(slab), width)
+        project(pre_a, 0, slab_columns(slab + 1), width)
+        activate(pre_b, 1, slab_columns(slab), width)
+
+        @pl.when(slab == 0)
+        def _():
+            img_wait(1)
+            img_start(2)
+
+        @pl.when(slab == 2)
+        def _():
+            img_wait(2)
+            img_start(3)
+
+    end = slice(last - width, last)
+    project(pre_b, 1, end, width)
+    activate(pre_a, 0, end, width)
+    if last < hidden:
+        rest = slice(last, hidden)
+        slope_ref[:, last:] = jnp.zeros((tokens, slope_ref.shape[1] - last), f32)
+        project(pre_a, 0, rest, hidden - last)
+        activate(pre_b, 1, end, width)
+        project(pre_b, 1, rest, hidden - last)
+        activate(pre_a, 0, rest, hidden - last)
+        activate(pre_b, 1, rest, hidden - last)
+    else:
+        activate(pre_b, 1, end, width)
+
+    gbar_ref[...] = gmean[:, :hidden].astype(bf16)
+    down_copy.wait()
+    mine[...] = lax.dot_general(
+        gbar_ref[...], w_down[...], (((1,), (1,)), ((), ())), preferred_element_type=f32
+    )
+    mp_copy = remote(mine, theirs, mp_sems, 0, place.mp_peer())
+    mp_copy.start()
+    for turn in range(2):
+        own_t[:, turn * tile : (turn + 1) * tile] = normed[turn * tile : (turn + 1) * tile, :].T
+    t_copy = remote(own_t, other_t, t_sems, 0, place.peer(*core))
+    t_copy.start()
+    img_wait(3)
+    mp_copy.wait_recv()
+    pooled = tmean[...] + (mine[...] + theirs[...])
+    unit_text, text_scale = unit_rows(pooled)
+    text_half = unit_text.astype(bf16)
+    text_ref[...] = text_half
+    signs, signed = signed_logits(text_half, own_group_ref[...], images[...], group_ref[...])
+    loss = jnp.sum(jnp.maximum(-signed, 0.0) + jnp.log1p(jnp.exp(-jnp.abs(signed))), 1, keepdims=True)
+    loss_ref[...] = jnp.broadcast_to(loss / total, loss_ref.shape)
+    text_back = jnp.dot(loss_slope(signs, signed), images[...], preferred_element_type=f32)
+    pooled_half = through_unit(text_back, unit_text, text_scale).astype(bf16)
+    pooled_ref[...] = pooled_half
+    hidden_ref[:, last:] = jnp.zeros((captions, hidden_ref.shape[1] - last), f32)
+    hidden_ref[:, :hidden] = jnp.dot(pooled_half, w_down[...], preferred_element_type=f32)
+
+    for stage in range(4):
+        for c in img_copies(stage):
+            c.wait_send()
+    mp_copy.wait_send()
+    t_copy.wait()
+
+
+def forward(tokens, share, images, pair_group, own_group, w_up, w_down, total):
+    count, width = tokens.shape
+    captions = images.shape[0]
+    hidden = w_up.shape[1]
+    slab = slab_width(hidden)
+    bf16, f32 = jnp.bfloat16, jnp.float32
+    vmem = pl.BlockSpec(memory_space=pltpu.VMEM)
+    hbm = pl.BlockSpec(memory_space=pl.ANY)
+    dma = pltpu.SemaphoreType.DMA
+    shape = jax.ShapeDtypeStruct
+    return pl.pallas_call(
+        functools.partial(forward_kernel, total),
+        out_shape=(
+            shape((captions, hidden), bf16),
+            shape((captions, width), bf16),
+            shape((captions, width), bf16),
+            shape((captions, LANES), f32),
+            shape((captions, 2 * SLABS * slab), f32),
+            shape((count, 2 * SLABS * slab), f32),
+            shape((width, count), bf16),
+            shape((width, count), bf16),
+        ),
+        in_specs=[vmem] * 5 + [hbm] * 2,
+        out_specs=(vmem,) * 8,
+        scratch_shapes=[
+            pltpu.VMEM(w_up.shape, bf16),
+            pltpu.VMEM(w_down.shape, bf16),
+            pltpu.VMEM((count, width), bf16),
+            pltpu.VMEM((count // 2, slab), f32),
+            pltpu.VMEM((count // 2, slab), f32),
+            pltpu.VMEM((captions, 2 * SLABS * slab), f32),
+            pltpu.VMEM((captions, width), f32),
+            pltpu.VMEM((total, width), bf16),
+            pltpu.VMEM((captions, width), f32),
+            pltpu.VMEM((captions, width), f32),
+            dma((2,)),
+            dma((2, 15)),
+            dma((2, 1)),
+            dma((2, 1)),
+        ],
+        cost_estimate=pl.CostEstimate(
+            flops=2 * count * width * hidden, bytes_accessed=4 * count * hidden,
+            transcendentals=count * hidden,
+        ),
+        compiler_params=pltpu.CompilerParams(
+            collective_id=1, has_side_effects=True, vmem_limit_bytes=56 * 1024 * 1024
+        ),
+    )(
+        tokens,
+        share,
+        images,
+        pair_group.reshape(1, total),
+        own_group.reshape(captions, 1),
+        w_up,
+        w_down,
+    )
+
+
 def sum_over_chips_kernel(
-    own_ref, other_ref, grad_ref, out_ref, grad_other, keep, x_out, x_in, near_out, near_in,
+    own_ref, other_ref, hidden_ref, share_ref, slope_ref, out_ref, grad_ref, grad_other, keep, x_out, x_in, near_out, near_in,
     far_out, far_in, swap_out, swap_in, grad_sems, x_sems, near_sems, far_sems, swap_sems
 ):
     rank = lax.axis_index("dp")
@@ -98,8 +367,28 @@
     def swap_copy(step):
         return copy(swap_out.at[step], swap_in.at[step], swap_sems, step, core_peer)
 
-    for slab in range(SLABS):
+    tokens = grad_ref.shape[0]
+    captions = hidden_ref.shape[0]
+    tile, tile_captions = tokens // 2, captions // 2
+
+    def make_grad(which, slab):
+        cols = columns(which, slab)
+        for turn in range(2):
+            at = slice(turn * tile, (turn + 1) * tile)
+            of = slice(turn * tile_captions, (turn + 1) * tile_captions)
+            shape = (tile_captions, tokens // captions, width)
+            hidden = jnp.broadcast_to(hidden_ref[of, cols][:, None, :], shape).reshape(tile, width)
+            grad = share_ref[at, 0:1] * hidden * slope_ref[at, cols]
+            grad_ref[at, cols] = grad.astype(jnp.bfloat16)
+
+    @pl.loop(0, SLABS)
+    def _(slab):
+        make_grad(1 - core, slab)
         grad_copy(slab).start()
+
+    @pl.loop(0, SLABS)
+    def _(slab):
+        make_grad(core, slab)
 
     def block(d0, d1, x_at, slab):
         z_at = z + d0 * (1 - 2 * low) + d1 * (2 - 4 * high)
@@ -186,21 +475,22 @@
         near_copy(step).wait_send()
 
 
-def sum_over_chips(own_t, other_t, pre_grad):
+def sum_over_chips(own_t, other_t, hidden_grad, share, slope):
     features, tokens = own_t.shape
-    width = pre_grad.shape[1] // (2 * SLABS)
+    width = slope.shape[1] // (2 * SLABS)
     rows = features // 8
     own_rows = rows // 2
     bf16, f32 = jnp.bfloat16, jnp.float32
     vmem = pl.BlockSpec(memory_space=pltpu.VMEM)
     dma = pltpu.SemaphoreType.DMA
-    flops = 4 * features * tokens * pre_grad.shape[1] // 2
+    flops = 4 * features * tokens * slope.shape[1] // 2
     return pl.pallas_call(
         sum_over_chips_kernel,
-        out_shape=jax.ShapeDtypeStruct((own_rows, pre_grad.shape[1]), f32),
-        in_specs=[vmem] * 3,
+        out_shape=jax.ShapeDtypeStruct((own_rows, slope.shape[1]), f32),
+        in_specs=[vmem] * 5,
         out_specs=vmem,
         scratch_shapes=[
+            pltpu.VMEM(slope.shape, bf16),
             pltpu.VMEM((SLABS, tokens, width), bf16),
             pltpu.VMEM((4, SLABS, rows, width), f32),
             pltpu.VMEM((4 * SLABS, rows, width), bf16),
@@ -218,32 +508,12 @@
             dma((2, SLABS)),
         ],
         cost_estimate=pl.CostEstimate(
-            flops=flops, bytes_accessed=4 * features * pre_grad.shape[1], transcendentals=0
+            flops=flops, bytes_accessed=4 * features * slope.shape[1], transcendentals=0
         ),
         compiler_params=pltpu.CompilerParams(
-            collective_id=0, has_side_effects=True, vmem_limit_bytes=48 * 1024 * 1024
+            collective_id=0, has_side_effects=True, vmem_limit_bytes=56 * 1024 * 1024
         ),
-    )(own_t, other_t, pre_grad)
-
-
-def signed_logits(text_rows, text_group, image_rows, image_group):
-    logits = (
-        LOGIT_SCALE
-        * lax.dot_general(
-            text_rows, image_rows, (((1,), (1,)), ((), ())), preferred_element_type=jnp.float32
-        )
-        + LOGIT_SHIFT
-    )
-    signs = jnp.where(text_group[:, None] == image_group[None, :], 1.0, -1.0).astype(jnp.float32)
-    return (signs, signs * logits)
-
-
-def loss_slope(signs, signed):
-    return (-LOGIT_SCALE * signs * jax.nn.sigmoid(-signed)).astype(jnp.bfloat16)
-
-
-def through_unit(back, unit, scale):
-    return (back - unit * jnp.sum(unit * back, 1, keepdims=True)) * scale
+    )(own_t, other_t, hidden_grad, share, slope)
 
 
 def on_device(tokens, lengths, images, pair_group, w_up, w_down):
@@ -256,33 +526,42 @@
     total = captions * devices
     own_rows = width // devices
     own_group = lax.dynamic_slice_in_dim(pair_group, own_index * captions, captions)
-
-    unit_image, image_scale = unit_rows(images.astype(jnp.float32))
-    image_half = unit_image.astype(jnp.bfloat16)
-    all_images = lax.all_gather(unit_image, "dp", axis=0, tiled=True)
-    all_images = lax.optimization_barrier(all_images).astype(jnp.bfloat16)
-
-    tok_float = tokens.astype(jnp.float32)
-    normed = layer_norm(tok_float).astype(jnp.bfloat16)
-    pre = jnp.dot(normed, w_up, preferred_element_type=jnp.float32)
-    value, slope = gelu_pair(pre)
     position = jnp.arange(seq_len, dtype=jnp.int32)
     valid = (position[None, :] < lengths[:, None]).astype(jnp.float32)
     share = valid / jnp.sum(valid, 1, keepdims=True)
-    gmean = jnp.sum(value.reshape(captions, seq_len, hidden) * share[:, :, None], 1)
-    tmean = jnp.sum(tok_float.reshape(captions, seq_len, width) * share[:, :, None], 1)
-    gbar = gmean.astype(jnp.bfloat16)
-    partial_value = lax.dot_general(
-        gbar, w_down, (((1,), (1,)), ((), ())), preferred_element_type=jnp.float32
-    )
-    pooled = tmean + lax.psum(partial_value, "mp")
-    unit_text, text_scale = unit_rows(pooled)
-    text_half = unit_text.astype(jnp.bfloat16)
-
-    signs, signed = signed_logits(text_half, own_group, all_images, pair_group)
-    caption_loss = -jnp.sum(jax.nn.log_sigmoid(signed), 1) / total
-    text_back = jnp.dot(loss_slope(signs, signed), all_images, preferred_element_type=jnp.float32)
-    pooled_half = through_unit(text_back, unit_text, text_scale).astype(jnp.bfloat16)
+    unit_image, image_scale = unit_rows(images.astype(jnp.float32))
+    image_half = unit_image.astype(jnp.bfloat16)
+
+    by_chips = devices == 16 and lax.axis_size("mp") == 2 and captions == 16
+    if by_chips:
+        share = jnp.broadcast_to(share.reshape(captions * seq_len, 1), (captions * seq_len, LANES))
+        gbar, text_half, pooled_half, loss, hidden_grad, slope, own_t, other_t = forward(
+            tokens, share, images, pair_group, own_group, w_up, w_down, total
+        )
+        caption_loss = loss[:, 0]
+    else:
+        all_images = lax.all_gather(image_half, "dp", axis=0, tiled=True)
+        tok_float = tokens.astype(jnp.float32)
+        normed = layer_norm(tok_float).astype(jnp.bfloat16)
+        pre = jnp.dot(normed, w_up, preferred_element_type=jnp.float32)
+        value, slope = gelu_pair(pre)
+        gmean = jnp.sum(value.reshape(captions, seq_len, hidden) * share[:, :, None], 1)
+        tmean = jnp.sum(tok_float.reshape(captions, seq_len, width) * share[:, :, None], 1)
+        gbar = gmean.astype(jnp.bfloat16)
+        partial_value = lax.dot_general(
+            gbar, w_down, (((1,), (1,)), ((), ())), preferred_element_type=jnp.float32
+        )
+        pooled = tmean + lax.psum(partial_value, "mp")
+        unit_text, text_scale = unit_rows(pooled)
+        text_half = unit_text.astype(jnp.bfloat16)
+        signs, signed = signed_logits(
+            text_half, own_group[:, None], all_images, pair_group[None, :]
+        )
+        caption_loss = -jnp.sum(jax.nn.log_sigmoid(signed), 1) / total
+        text_back = jnp.dot(
+            loss_slope(signs, signed), all_images, preferred_element_type=jnp.float32
+        )
+        pooled_half = through_unit(text_back, unit_text, text_scale).astype(jnp.bfloat16)
 
     gathered = lax.all_gather(
         jnp.concatenate([text_half, pooled_half, gbar], 1), "dp", axis=0, tiled=True
@@ -291,21 +570,14 @@
     all_pooled = gathered[:, width : 2 * width]
     all_gbar = gathered[:, 2 * width :]
 
-    by_chips = devices == 16 and width % 128 == 0
     if by_chips:
-        padding = 2 * SLABS * slab_width(hidden) - hidden
-        w_down = jnp.pad(w_down, ((0, 0), (0, padding)))
-        slope = jnp.pad(slope, ((0, 0), (0, padding)))
-    hidden_grad = jnp.dot(pooled_half, w_down, preferred_element_type=jnp.float32)
-    pre_grad = (
-        share[:, :, None] * hidden_grad[:, None, :] * slope.reshape(captions, seq_len, -1)
-    ).astype(jnp.bfloat16)
-    pre_grad = pre_grad.reshape(captions * seq_len, -1)
-    if by_chips:
-        normed_t = normed.T
-        other_t = lax.ppermute(normed_t, "dp", [(i, i ^ 1) for i in range(devices)])
-        up_grad = sum_over_chips(normed_t, other_t, pre_grad)[:, :hidden]
+        up_grad = sum_over_chips(own_t, other_t, hidden_grad, share, slope)[:, :hidden]
     else:
+        hidden_grad = jnp.dot(pooled_half, w_down, preferred_element_type=jnp.float32)
+        pre_grad = (
+            share[:, :, None] * hidden_grad[:, None, :] * slope.reshape(captions, seq_len, hidden)
+        ).astype(jnp.bfloat16)
+        pre_grad = pre_grad.reshape(captions * seq_len, hidden)
         up_grad = lax.psum_scatter(
             lax.dot_general(
                 normed, pre_grad, (((0,), (0,)), ((), ())), preferred_element_type=jnp.float32
@@ -315,7 +587,9 @@
             tiled=True,
         )
 
-    signs, signed = signed_logits(all_texts, pair_group, image_half, own_group)
+    signs, signed = signed_logits(
+        all_texts, pair_group[:, None], image_half, own_group[None, :]
+    )
     image_back = lax.dot_general(
         loss_slope(signs, signed), all_texts, (((0,), (0,)), ((), ())),
         preferred_element_type=jnp.float32,

time: 142 us -> 135 us (0.951)
  Pallas kernels: 49.5 us -> 91 us
  blocking collectives: 25 us -> 0 us
  matrix products: 23 us -> 3.36 us
  other arithmetic: 20.3 us -> 3.99 us
  local copies, waits for them, and re-layouts: 8.11 us -> 22 us
    pallas_call x0 -> x1, Pallas kernels: none -> 34.5 us  [forward(): pl.pallas_call(functools.partial(forward_kernel, total), out_shape=(shape...]
    all_gather x1 -> x0, blocking collectives: 25 us -> none  [on_device(): all_images = lax.all_gather(unit_image, 'dp', axis=0, tiled=True)]
    dot_general x5 -> x0, matrix products: 18.5 us -> none  [the longest x1 12.5 us: on_device(): pre = jnp.dot(normed, w_up, preferred_element_type=jnp.float32)]
    unnamed x13 -> x10, local copies, waits for them, and re-layouts: 2.87 us -> 16.8 us
    add x1 -> x0, other arithmetic: 7.26 us -> none  [gelu_pair(): 0.5 * (1.0 + tanh_u)]
    pallas_call x1, Pallas kernels: 49.5 us -> 56.5 us  [sum_over_chips(): pl.pallas_call(sum_over_chips_kernel, out_shape=jax.ShapeDtypeStruct((own...]
    reduce_sum x3 -> x0, other arithmetic: 4.06 us -> none  [the longest x1 3 us: on_device(): jnp.sum(tok_float.reshape(captions, seq_len, width) * share[:, :, None], 1)]
    convert_element_type x3 -> x0, other arithmetic: 3.18 us -> none  [the longest x1 3.01 us: on_device(): pre_grad = (share[:, :, None] * hidden_grad[:, None, :] * slope.reshape(c...]
  transfers between devices with their start and end apart: 3 -> 1, of which waited for: 0 -> 0; matrix products, arithmetic and copies ran while one was open for 17% -> 2% of each run, Pallas kernels for 35% -> 42%
where the time goes in v3:
time: 135 us
  Pallas kernels  91 us (67%)
  local copies, waits for them, and re-layouts  22 us (16%)
  between operations  14.1 us (10%)
  other arithmetic  3.99 us (3%)
  matrix products  3.36 us (2%)
    pallas_call x1, Pallas kernels, sum_over_chips(): pl.pallas_call(sum_over_chips_kernel, out_shape=jax.ShapeDtypeStruct((own...  56.5 us
    pallas_call x1, Pallas kernels, forward(): pl.pallas_call(functools.partial(forward_kernel, total), out_shape=(shape...  34.5 us
    unnamed x10, local copies, waits for them, and re-layouts  16.8 us
  transfers between devices with their start and end apart: 1, of which 0 were waited for; matrix products, arithmetic and copies ran while one was open for 2% of the time, Pallas kernels for 42%

profile of v3, /device:TPU:0, one launch (start us, length us, event | category | flops | bytes accessed | tf_op | source)
XLA Modules:
  0.0 134.5 jit_solution(16747359521422356201)
XLA Ops:
  7.2 0.0 all-gather.2.cloned.1.call-start
  7.2 0.8 dynamic-slice_bitcast_fusion
  8.0 0.7 copy.16.own_group_ref
  8.7 0.8 convert_reduce_fusion
  9.5 0.7 convert_divide_fusion
  10.2 0.1 div.20
  10.3 8.4 %copy.17.up_hbm = bf16[1152,2152]{1,0:T(8,128)(2,1)} copy(bf16[1152,2152]{0,1:T(8,128)(2,1)} %param.10) | data formatting | bytes 9916416 | tf_op args[4]
  18.7 8.4 %copy.18.down_hbm = bf16[1152,2152]{1,0:T(8,128)(2,1)} copy(bf16[1152,2152]{0,1:T(8,128)(2,1)} %param.11) | data formatting | bytes 9916416 | tf_op args[5]
  27.1 1.0 broadcast_in_dim.8.share_ref
  28.1 0.0 copy-start.3
  28.1 34.5 %shard_map.93 = (bf16[16,2152]{1,0:T(8,128)(2,1)}, bf16[16,1152]{1,0:T(8,128)(2,1)}, bf16[16,1152]{1,0:T(8,128)(2,1)}, f32[16,128]{1,0:T(8,128)}, f32[16,2304]{1...) custom-call(bf16[1024,1152]{1,0:T(8,128)(2,1)} %tok_ref.1, ...), custom_call_target="tpu_custom_call" | custom-call | flops 5077204992 | bytes 8814592 | tf_op jit(solution)/shard_map/pallas_call | solution.py:264
  62.6 1.6 %pad_maximum_fusion = bf16[16,4456]{1,0:T(8,128)(2,1)} fusion(bf16[16,2152]{1,0:T(8,128)(2,1)} %get-tuple-element.15, bf16[16,1152]{1,0:T(8,128)(2,1)} %get-tuple-element.14, bf16[16,1152]{1,0:T(8,128)(2,1)} %get-tuple-element.13), kind=kLoop, calls=%fused_computation.12 | loop fusion | flops 427776 | bytes 285184 | tf_op jit(solution)/shard_map/concatenate | solution.py:567
  64.2 0.0 all-gather.2.cloned.1.call-update
  64.2 0.0 copy-done.3
  64.2 0.1 dynamic_slice.6
  64.3 0.0 copy-start.2
  64.3 0.0 copy-start.1
  64.3 56.5 %shard_map.94 = f32[72,2304]{1,0:T(8,128)} custom-call(bf16[1152,1024]{1,0:T(8,128)(2,1)} %get-tuple-element.16.own_ref, bf16[1152,1024]{1,0:T(8,128)(2,1)} %get-tuple-element.17.other_ref, f32[16,2304]{1,0:T(8,128)} %get-tuple-element.18.hidden_ref, f32[1024,128]{1,0:T(8,128)} %broadcast_in_dim.8.share_ref, f32[1024,2304]{1,0:T(8,128)} %get-tuple-element.19.slope_ref), custom_call_target="tpu_custom_call" | custom-call | flops 5435817984 | bytes 10616832 | tf_op jit(solution)/shard_map/pallas_call | solution.py:487
  120.8 1.9 %slice.17 = f32[72,2152]{1,0:T(8,128)} slice(f32[72,2304]{1,0:T(8,128)} %shard_map.94), slice={[0:72], [0:2152]} | slice | bytes 1239552 | tf_op jit(solution)/shard_map/slice | solution.py:574
  122.8 0.0 copy-done.2
  122.8 0.6 slice_reduce_fusion
  123.4 0.0 copy-done.1
  123.4 0.1 fusion.18
  123.5 0.0 all-gather.2.cloned.1.call-done
  123.5 0.0 copy-start
  123.6 0.0 slice-start
  123.6 2.1 %fusion.15 = (f32[16]{0:T(128)S(1)}, f32[16,1152]{1,0:T(8,128)S(1)}) fusion(bf16[16,1152]{1,0:T(8,128)(2,1)S(1)} %copy-done.1, f32[16]{0:T(128)S(1)} %add_rsqrt_fusion, bf16[256,4456]{1,0:T(8,128)(2,1)} %all-gather.2.cloned.1.call-done, s32[256]{0:T(256)S(1)} %copy-done.3, s32[16]{0:T(128)S(1)} %dynamic_slice.6), kind=kOutput, calls=%fused_computation.18 | convolution fusion | flops 19044336 | bytes 1329728 | tf_op jit(solution)/shard_map/dot_general | solution.py:593
  125.7 0.7 fusion.17
  126.4 0.0 copy-done
  126.4 0.0 slice-done
  126.4 1.2 fusion
  (1 shorter events, 0.0 us)
Async XLA Ops:
  7.2 116.4 %all-gather.2.cloned.1.call-start = ((), (), s32[]{:S(2)}) async-start(), calls=%async_computation | async-start | bytes 2437120 | tf_op jit(solution)/shard_map/all_gather | solution.py:566
  28.1 36.1 %copy-start.3 = (s32[256]{0:T(256)S(1)}, s32[256]{0:T(256)}, u32[]{:S(2)}) copy-start(s32[256]{0:T(256)} %param.9) | copy-start | bytes 3076
  64.3 58.5 %copy-start.2 = (f32[16,128]{1,0:T(8,128)S(1)}, f32[16,128]{1,0:T(8,128)}, u32[]{:S(2)}) copy-start(f32[16,128]{1,0:T(8,128)} %get-tuple-element.12) | copy-start | bytes 24580
  64.3 59.1 %copy-start.1 = (bf16[16,1152]{1,0:T(8,128)(2,1)S(1)}, bf16[16,1152]{1,0:T(8,128)(2,1)}, u32[]{:S(2)}) copy-start(bf16[16,1152]{1,0:T(8,128)(2,1)} %img_ref.1) | copy-start | bytes 110596
  123.5 2.9 %copy-start = (bf16[256,4456]{1,0:T(8,128)(2,1)S(1)}, bf16[256,4456]{1,0:T(8,128)(2,1)}, u32[]{:S(2)}) copy-start(bf16[256,4456]{1,0:T(8,128)(2,1)} %all-gather.2.cloned.1.call-done) | copy-start | bytes 6844420
  123.6 2.9 %slice-start = ((bf16[256,4456]{1,0:T(8,128)(2,1)}), bf16[256,1152]{1,0:T(8,128)(2,1)S(1)}, s32[]{:S(2)}) async-start(bf16[256,4456]{1,0:T(8,128)(2,1)} %all-gather.2.cloned.1.call-done), calls=%async_computation.1 | async-start | bytes 1179648 | tf_op jit(solution)/shard_map/slice | solution.py:570
Sparse Core Ops, SparseCore 0:
  64.3 52.1 all-gather.1

commit v4 on v3

--- a/solution.py
+++ b/solution.py
@@ -171,8 +171,9 @@
     up_copy.wait()
 
     def project(dst, turn, cols, size):
-        dst[:, :size] = jnp.dot(
-            normed[turn * tile : (turn + 1) * tile, :], w_up[:, cols], preferred_element_type=f32
+        dst[:, :size] = lax.dot_general(
+            normed[turn * tile : (turn + 1) * tile, :], w_up[cols, :], (((1,), (1,)), ((), ())),
+            preferred_element_type=f32,
         )
 
     def activate(src, turn, cols, size):
@@ -220,9 +221,7 @@
 
     gbar_ref[...] = gmean[:, :hidden].astype(bf16)
     down_copy.wait()
-    mine[...] = lax.dot_general(
-        gbar_ref[...], w_down[...], (((1,), (1,)), ((), ())), preferred_element_type=f32
-    )
+    mine[...] = jnp.dot(gbar_ref[...], w_down[...], preferred_element_type=f32)
     mp_copy = remote(mine, theirs, mp_sems, 0, place.mp_peer())
     mp_copy.start()
     for turn in range(2):
@@ -242,7 +241,9 @@
     pooled_half = through_unit(text_back, unit_text, text_scale).astype(bf16)
     pooled_ref[...] = pooled_half
     hidden_ref[:, last:] = jnp.zeros((captions, hidden_ref.shape[1] - last), f32)
-    hidden_ref[:, :hidden] = jnp.dot(pooled_half, w_down[...], preferred_element_type=f32)
+    hidden_ref[:, :hidden] = lax.dot_general(
+        pooled_half, w_down[...], (((1,), (1,)), ((), ())), preferred_element_type=f32
+    )
 
     for stage in range(4):
         for c in img_copies(stage):
@@ -254,7 +255,7 @@
 def forward(tokens, share, images, pair_group, own_group, w_up, w_down, total):
     count, width = tokens.shape
     captions = images.shape[0]
-    hidden = w_up.shape[1]
+    hidden = w_up.shape[0]
     slab = slab_width(hidden)
     bf16, f32 = jnp.bfloat16, jnp.float32
     vmem = pl.BlockSpec(memory_space=pltpu.VMEM)
@@ -536,7 +537,7 @@
     if by_chips:
         share = jnp.broadcast_to(share.reshape(captions * seq_len, 1), (captions * seq_len, LANES))
         gbar, text_half, pooled_half, loss, hidden_grad, slope, own_t, other_t = forward(
-            tokens, share, images, pair_group, own_group, w_up, w_down, total
+            tokens, share, images, pair_group, own_group, w_up.T, w_down.T, total
         )
         caption_loss = loss[:, 0]
     else:

time: 135 us -> 117 us (0.87)
  local copies, waits for them, and re-layouts: 22 us -> 5.18 us
    unnamed x10 -> x8, local copies, waits for them, and re-layouts: 16.8 us -> 0.02 us
  transfers between devices with their start and end apart: 1 -> 1, of which waited for: 0 -> 0; matrix products, arithmetic and copies ran while one was open for 2% -> 2% of each run, Pallas kernels for 42% -> 48%
where the time goes in v4:
time: 117 us
  Pallas kernels  90.4 us (77%)
  between operations  14.1 us (12%)
  local copies, waits for them, and re-layouts  5.18 us (4%)
  other arithmetic  3.98 us (3%)
  matrix products  3.36 us (3%)
    pallas_call x1, Pallas kernels, sum_over_chips(): pl.pallas_call(sum_over_chips_kernel, out_shape=jax.ShapeDtypeStruct((own...  56.6 us
    pallas_call x1, Pallas kernels, forward(): pl.pallas_call(functools.partial(forward_kernel, total), out_shape=(shape...  33.8 us
  transfers between devices with their start and end apart: 1, of which 0 were waited for; matrix products, arithmetic and copies ran while one was open for 2% of the time, Pallas kernels for 48%

profile of v4, /device:TPU:0, one launch (start us, length us, event | category | flops | bytes accessed | tf_op | source)
XLA Modules:
  0.0 117.1 jit_solution(2676689128594246684)
XLA Ops:
  7.2 0.0 all-gather.2.cloned.1.call-start
  7.2 0.8 convert_reduce_fusion
  8.1 0.8 dynamic-slice_bitcast_fusion
  8.8 0.7 copy.12.own_group_ref
  9.5 0.7 convert_divide_fusion
  10.2 0.1 div.20
  10.3 1.0 broadcast_in_dim.8.share_ref
  11.3 0.0 copy-start.3
  11.3 33.8 %shard_map.93 = (bf16[16,2152]{1,0:T(8,128)(2,1)}, bf16[16,1152]{1,0:T(8,128)(2,1)}, bf16[16,1152]{1,0:T(8,128)(2,1)}, f32[16,128]{1,0:T(8,128)}, f32[16,2304]{1...) custom-call(bf16[1024,1152]{1,0:T(8,128)(2,1)} %tok_ref.1, ...), custom_call_target="tpu_custom_call" | custom-call | flops 5077204992 | bytes 8814592 | tf_op jit(solution)/shard_map/pallas_call | solution.py:265
  45.1 1.6 %pad_maximum_fusion = bf16[16,4456]{1,0:T(8,128)(2,1)} fusion(bf16[16,2152]{1,0:T(8,128)(2,1)} %get-tuple-element.15, bf16[16,1152]{1,0:T(8,128)(2,1)} %get-tuple-element.14, bf16[16,1152]{1,0:T(8,128)(2,1)} %get-tuple-element.13), kind=kLoop, calls=%fused_computation.12 | loop fusion | flops 427776 | bytes 285184 | tf_op jit(solution)/shard_map/concatenate | solution.py:568
  46.7 0.0 all-gather.2.cloned.1.call-update
  46.7 0.0 copy-done.3
  46.7 0.1 dynamic_slice.6
  46.8 0.0 copy-start.2
  46.8 0.0 copy-start.1
  46.8 56.6 %shard_map.94 = f32[72,2304]{1,0:T(8,128)} custom-call(bf16[1152,1024]{1,0:T(8,128)(2,1)} %get-tuple-element.16.own_ref, bf16[1152,1024]{1,0:T(8,128)(2,1)} %get-tuple-element.17.other_ref, f32[16,2304]{1,0:T(8,128)} %get-tuple-element.18.hidden_ref, f32[1024,128]{1,0:T(8,128)} %broadcast_in_dim.8.share_ref, f32[1024,2304]{1,0:T(8,128)} %get-tuple-element.19.slope_ref), custom_call_target="tpu_custom_call" | custom-call | flops 5435817984 | bytes 10616832 | tf_op jit(solution)/shard_map/pallas_call | solution.py:488
  103.4 1.9 %slice.17 = f32[72,2152]{1,0:T(8,128)} slice(f32[72,2304]{1,0:T(8,128)} %shard_map.94), slice={[0:72], [0:2152]} | slice | bytes 1239552 | tf_op jit(solution)/shard_map/slice | solution.py:575
  105.3 0.0 copy-done.2
  105.3 0.6 slice_reduce_fusion
  105.9 0.0 copy-done.1
  105.9 0.1 fusion.18
  106.1 0.0 all-gather.2.cloned.1.call-done
  106.1 0.0 copy-start
  106.1 0.0 slice-start
  106.1 2.1 %fusion.15 = (f32[16]{0:T(128)S(1)}, f32[16,1152]{1,0:T(8,128)S(1)}) fusion(bf16[16,1152]{1,0:T(8,128)(2,1)S(1)} %copy-done.1, f32[16]{0:T(128)S(1)} %add_rsqrt_fusion, bf16[256,4456]{1,0:T(8,128)(2,1)} %all-gather.2.cloned.1.call-done, s32[256]{0:T(256)S(1)} %copy-done.3, s32[16]{0:T(128)S(1)} %dynamic_slice.6), kind=kOutput, calls=%fused_computation.18 | convolution fusion | flops 19044336 | bytes 1329728 | tf_op jit(solution)/shard_map/dot_general | solution.py:594
  108.2 0.7 fusion.17
  109.0 0.0 copy-done
  109.0 0.0 slice-done
  109.0 1.2 %fusion = f32[72,2152]{1,0:T(8,128)} fusion(bf16[256,4456]{1,0:T(8,128)(2,1)S(1)} %copy-done, bf16[256,1152]{1,0:T(8,128)(2,1)S(1)} %slice-done, s32[]{:T(128)S(6)} %select_n.12), kind=kOutput, calls=%fused_computation | convolution fusion | flops 79331328 | bytes 1799428 | tf_op jit(solution)/shard_map/dot_general | solution.py:600
  (1 shorter events, 0.0 us)
Async XLA Ops:
  7.2 98.9 %all-gather.2.cloned.1.call-start = ((), (), s32[]{:S(2)}) async-start(), calls=%async_computation | async-start | bytes 2437120 | tf_op jit(solution)/shard_map/all_gather | solution.py:567
  11.3 35.4 %copy-start.3 = (s32[256]{0:T(256)S(1)}, s32[256]{0:T(256)}, u32[]{:S(2)}) copy-start(s32[256]{0:T(256)} %param.9) | copy-start | bytes 3076
  46.8 58.5 %copy-start.2 = (f32[16,128]{1,0:T(8,128)S(1)}, f32[16,128]{1,0:T(8,128)}, u32[]{:S(2)}) copy-start(f32[16,128]{1,0:T(8,128)} %get-tuple-element.12) | copy-start | bytes 24580
  46.8 59.1 %copy-start.1 = (bf16[16,1152]{1,0:T(8,128)(2,1)S(1)}, bf16[16,1152]{1,0:T(8,128)(2,1)}, u32[]{:S(2)}) copy-start(bf16[16,1152]{1,0:T(8,128)(2,1)} %img_ref.1) | copy-start | bytes 110596
  106.1 2.9 %copy-start = (bf16[256,4456]{1,0:T(8,128)(2,1)S(1)}, bf16[256,4456]{1,0:T(8,128)(2,1)}, u32[]{:S(2)}) copy-start(bf16[256,4456]{1,0:T(8,128)(2,1)} %all-gather.2.cloned.1.call-done) | copy-start | bytes 6844420
  106.1 2.9 %slice-start = ((bf16[256,4456]{1,0:T(8,128)(2,1)}), bf16[256,1152]{1,0:T(8,128)(2,1)S(1)}, s32[]{:S(2)}) async-start(bf16[256,4456]{1,0:T(8,128)(2,1)} %all-gather.2.cloned.1.call-done), calls=%async_computation.1 | async-start | bytes 1179648 | tf_op jit(solution)/shard_map/slice | solution.py:571
Sparse Core Ops, SparseCore 0:
  46.8 52.2 all-gather.1

commit v5 on v4

--- a/solution.py
+++ b/solution.py
@@ -101,15 +101,19 @@
     )
 
 
-def forward_kernel(
-    total, tok_ref, share_ref, img_ref, group_ref, own_group_ref, up_hbm, down_hbm,
-    gbar_ref, text_ref, pooled_ref, loss_ref, hidden_ref, slope_ref, own_t, other_t,
+def whole_kernel(
+    total, tok_ref, share_ref, img_ref, group_ref, own_group_ref, group_col_ref, own_row_ref,
+    up_hbm, down_hbm,
+    loss_ref, img_grad_ref, out_ref, all_pooled, all_gbar,
+    all_text, hidden_ref, slope_ref, own_t, other_t,
     w_up, w_down, normed, pre_a, pre_b, gmean, tmean, images, mine, theirs,
-    local_sems, img_sems, mp_sems, t_sems
+    grad_ref, grad_other, keep, x_out, x_in, near_out, near_in, far_out, far_in, swap_out, swap_in,
+    local_sems, img_sems, mp_sems, t_sems, gbar_sems, text_sems, pooled_sems,
+    grad_sems, x_sems, near_sems, far_sems, swap_sems
 ):
     place = Place()
-    captions = gbar_ref.shape[0]
-    hidden = gbar_ref.shape[1]
+    captions = img_ref.shape[0]
+    hidden = w_up.shape[0]
     tokens = tok_ref.shape[0]
     seq_len = tokens // captions
     width = slab_width(hidden)
@@ -135,26 +139,36 @@
 
     stages = (far, near, across, core)
 
-    def img_copies(stage):
-        copies = []
-        for held in range(1 << stage):
-            flips = [(held >> bit) & 1 if bit < stage else 0 for bit in range(4)]
-            at = block_of(place.toward(*flips))
-            copies.append(
-                remote(images.at[at, :], images.at[at, :], img_sems, (1 << stage) - 1 + held,
-                       place.peer(*stages[stage]))
-            )
-        return copies
-
-    def img_start(stage):
-        for c in img_copies(stage):
-            c.start()
-
-    def img_wait(stage):
-        for c in img_copies(stage):
-            c.wait_recv()
-
-    img_start(0)
+    class Gather:
+        def __init__(self, ref, sems):
+            self.ref, self.sems = ref, sems
+
+        def copies(self, stage):
+            result = []
+            for held in range(1 << stage):
+                flips = [(held >> bit) & 1 if bit < stage else 0 for bit in range(4)]
+                part = self.ref.at[block_of(place.toward(*flips)), :]
+                index = (1 << stage) - 1 + held
+                result.append(remote(part, part, self.sems, index, place.peer(*stages[stage])))
+            return result
+
+        def start(self, stage):
+            for c in self.copies(stage):
+                c.start()
+
+        def wait(self, stage):
+            for c in self.copies(stage):
+                c.wait_recv()
+
+        def wait_sent(self):
+            for stage in range(4):
+                for c in self.copies(stage):
+                    c.wait_send()
+
+    img, gbars = Gather(images, img_sems), Gather(all_gbar, gbar_sems)
+    texts, pooleds = Gather(all_text, text_sems), Gather(all_pooled, pooled_sems)
+
+    img.start(0)
 
     @pl.loop(0, 2)
     def _(turn):
@@ -166,8 +180,8 @@
             shared, 1
         )
 
-    img_wait(0)
-    img_start(1)
+    img.wait(0)
+    img.start(1)
     up_copy.wait()
 
     def project(dst, turn, cols, size):
@@ -197,13 +211,13 @@
 
         @pl.when(slab == 0)
         def _():
-            img_wait(1)
-            img_start(2)
+            img.wait(1)
+            img.start(2)
 
         @pl.when(slab == 2)
         def _():
-            img_wait(2)
-            img_start(3)
+            img.wait(2)
+            img.start(3)
 
     end = slice(last - width, last)
     project(pre_b, 1, end, width)
@@ -219,134 +233,48 @@
     else:
         activate(pre_b, 1, end, width)
 
-    gbar_ref[...] = gmean[:, :hidden].astype(bf16)
+    gbar = gmean[:, :hidden].astype(bf16)
+    all_gbar[block_of(place.rank), :] = gbar
+    gbars.start(0)
     down_copy.wait()
-    mine[...] = jnp.dot(gbar_ref[...], w_down[...], preferred_element_type=f32)
+    mine[...] = jnp.dot(gbar, w_down[...], preferred_element_type=f32)
     mp_copy = remote(mine, theirs, mp_sems, 0, place.mp_peer())
     mp_copy.start()
     for turn in range(2):
         own_t[:, turn * tile : (turn + 1) * tile] = normed[turn * tile : (turn + 1) * tile, :].T
     t_copy = remote(own_t, other_t, t_sems, 0, place.peer(*core))
     t_copy.start()
-    img_wait(3)
+    gbars.wait(0)
+    gbars.start(1)
+    img.wait(3)
     mp_copy.wait_recv()
     pooled = tmean[...] + (mine[...] + theirs[...])
     unit_text, text_scale = unit_rows(pooled)
     text_half = unit_text.astype(bf16)
-    text_ref[...] = text_half
+    all_text[block_of(place.rank), :] = text_half
+    texts.start(0)
     signs, signed = signed_logits(text_half, own_group_ref[...], images[...], group_ref[...])
     loss = jnp.sum(jnp.maximum(-signed, 0.0) + jnp.log1p(jnp.exp(-jnp.abs(signed))), 1, keepdims=True)
     loss_ref[...] = jnp.broadcast_to(loss / total, loss_ref.shape)
     text_back = jnp.dot(loss_slope(signs, signed), images[...], preferred_element_type=f32)
     pooled_half = through_unit(text_back, unit_text, text_scale).astype(bf16)
-    pooled_ref[...] = pooled_half
+    all_pooled[block_of(place.rank), :] = pooled_half
+    pooleds.start(0)
+    gbars.wait(1)
+    gbars.start(2)
     hidden_ref[:, last:] = jnp.zeros((captions, hidden_ref.shape[1] - last), f32)
     hidden_ref[:, :hidden] = lax.dot_general(
         pooled_half, w_down[...], (((1,), (1,)), ((), ())), preferred_element_type=f32
     )
 
-    for stage in range(4):
-        for c in img_copies(stage):
-            c.wait_send()
-    mp_copy.wait_send()
-    t_copy.wait()
-
-
-def forward(tokens, share, images, pair_group, own_group, w_up, w_down, total):
-    count, width = tokens.shape
-    captions = images.shape[0]
-    hidden = w_up.shape[0]
-    slab = slab_width(hidden)
-    bf16, f32 = jnp.bfloat16, jnp.float32
-    vmem = pl.BlockSpec(memory_space=pltpu.VMEM)
-    hbm = pl.BlockSpec(memory_space=pl.ANY)
-    dma = pltpu.SemaphoreType.DMA
-    shape = jax.ShapeDtypeStruct
-    return pl.pallas_call(
-        functools.partial(forward_kernel, total),
-        out_shape=(
-            shape((captions, hidden), bf16),
-            shape((captions, width), bf16),
-            shape((captions, width), bf16),
-            shape((captions, LANES), f32),
-            shape((captions, 2 * SLABS * slab), f32),
-            shape((count, 2 * SLABS * slab), f32),
-            shape((width, count), bf16),
-            shape((width, count), bf16),
-        ),
-        in_specs=[vmem] * 5 + [hbm] * 2,
-        out_specs=(vmem,) * 8,
-        scratch_shapes=[
-            pltpu.VMEM(w_up.shape, bf16),
-            pltpu.VMEM(w_down.shape, bf16),
-            pltpu.VMEM((count, width), bf16),
-            pltpu.VMEM((count // 2, slab), f32),
-            pltpu.VMEM((count // 2, slab), f32),
-            pltpu.VMEM((captions, 2 * SLABS * slab), f32),
-            pltpu.VMEM((captions, width), f32),
-            pltpu.VMEM((total, width), bf16),
-            pltpu.VMEM((captions, width), f32),
-            pltpu.VMEM((captions, width), f32),
-            dma((2,)),
-            dma((2, 15)),
-            dma((2, 1)),
-            dma((2, 1)),
-        ],
-        cost_estimate=pl.CostEstimate(
-            flops=2 * count * width * hidden, bytes_accessed=4 * count * hidden,
-            transcendentals=count * hidden,
-        ),
-        compiler_params=pltpu.CompilerParams(
-            collective_id=1, has_side_effects=True, vmem_limit_bytes=56 * 1024 * 1024
-        ),
-    )(
-        tokens,
-        share,
-        images,
-        pair_group.reshape(1, total),
-        own_group.reshape(captions, 1),
-        w_up,
-        w_down,
-    )
-
-
-def sum_over_chips_kernel(
-    own_ref, other_ref, hidden_ref, share_ref, slope_ref, out_ref, grad_ref, grad_other, keep, x_out, x_in, near_out, near_in,
-    far_out, far_in, swap_out, swap_in, grad_sems, x_sems, near_sems, far_sems, swap_sems
-):
-    rank = lax.axis_index("dp")
-    column = lax.axis_index("mp")
-    core = rank % 2
-    x = (rank // 2) % 2
-    z = rank // 4
-    low, high = z % 2, z // 2
-    width = grad_other.shape[2]
+    core, x = place.core, place.x
+    low, high, z = place.low, place.high, place.z
+    core_peer, x_peer = place.peer(0, 0, 0, 1), place.peer(0, 0, 1, 0)
+    near_peer, far_peer = place.peer(0, 1, 0, 0), place.peer(1, 0, 0, 0)
     half = SLABS * width
     rows = keep.shape[2]
     own_rows = rows // 2
-
-    def device(z_at, x_at, core_at):
-        return ((z_at * 2 + x_at) * 2 + core_at, column)
-
-    core_peer = device(z, x, 1 - core)
-    x_peer = device(z, 1 - x, core)
-    near_peer = device(z + 1 - 2 * low, x, core)
-    far_peer = device(z + 2 - 4 * high, x, core)
-
-    barrier = pltpu.get_barrier_semaphore()
-    for peer in (core_peer, x_peer, near_peer, far_peer):
-        pl.semaphore_signal(barrier, inc=1, device_id=peer, device_id_type=MESH)
-    pl.semaphore_wait(barrier, 4)
-
-    def copy(src, dst, sems, index, peer):
-        return pltpu.make_async_remote_copy(
-            src_ref=src,
-            dst_ref=dst,
-            send_sem=sems.at[0, index],
-            recv_sem=sems.at[1, index],
-            device_id=peer,
-            device_id_type=MESH,
-        )
+    copy = remote
 
     def columns(which, slab):
         return pl.ds(pl.multiple_of(which * half + slab * width, LANES), width)
@@ -367,10 +295,6 @@
 
     def swap_copy(step):
         return copy(swap_out.at[step], swap_in.at[step], swap_sems, step, core_peer)
-
-    tokens = grad_ref.shape[0]
-    captions = hidden_ref.shape[0]
-    tile, tile_captions = tokens // 2, captions // 2
 
     def make_grad(which, slab):
         cols = columns(which, slab)
@@ -387,16 +311,27 @@
         make_grad(1 - core, slab)
         grad_copy(slab).start()
 
+    texts.wait(0)
+    texts.start(1)
+    pooleds.wait(0)
+    pooleds.start(1)
+
     @pl.loop(0, SLABS)
     def _(slab):
         make_grad(core, slab)
+
+    texts.wait(1)
+    texts.start(2)
+    pooleds.wait(1)
+    pooleds.start(2)
+    t_copy.wait_recv()
 
     def block(d0, d1, x_at, slab):
         z_at = z + d0 * (1 - 2 * low) + d1 * (2 - 4 * high)
         at = pl.ds(pl.multiple_of((z_at * 2 + x_at) * rows, 16), rows)
         return jnp.dot(
-            own_ref[at, :], grad_ref[:, columns(core, slab)], preferred_element_type=jnp.float32
-        ) + jnp.dot(other_ref[at, :], grad_other[slab], preferred_element_type=jnp.float32)
+            own_t[at, :], grad_ref[:, columns(core, slab)], preferred_element_type=jnp.float32
+        ) + jnp.dot(other_t[at, :], grad_other[slab], preferred_element_type=jnp.float32)
 
     for slab in range(SLABS):
         grad_copy(slab).wait_recv()
@@ -416,6 +351,9 @@
     def _(step):
         turn, slab = step // SLABS, step % SLABS
         keep[step // SLABS, step % SLABS] = block(1 - turn % 2, 1 - turn // 2, x, slab)
+
+    gbars.wait(2)
+    gbars.start(3)
 
     @pl.loop(0, SLABS)
     def _(slab):
@@ -442,6 +380,21 @@
         ).astype(jnp.bfloat16)
         near_copy(SLABS + slab).start()
 
+    texts.wait(2)
+    texts.start(3)
+    pooleds.wait(2)
+    pooleds.start(3)
+    unit_image, image_scale = unit_rows(img_ref[...].astype(f32))
+    texts.wait(3)
+    signs, signed = signed_logits(
+        all_text[...], group_col_ref[...], unit_image.astype(bf16), own_row_ref[...]
+    )
+    image_back = lax.dot_general(
+        loss_slope(signs, signed), all_text[...], (((0,), (0,)), ((), ())),
+        preferred_element_type=f32,
+    )
+    img_grad_ref[...] = through_unit(image_back, unit_image, image_scale)
+
     for slab in range(SLABS):
         x_copy(3 * SLABS + slab).wait_recv()
         near_copy(SLABS + slab).wait_recv()
@@ -475,33 +428,72 @@
     def _(step):
         near_copy(step).wait_send()
 
-
-def sum_over_chips(own_t, other_t, hidden_grad, share, slope):
-    features, tokens = own_t.shape
-    width = slope.shape[1] // (2 * SLABS)
-    rows = features // 8
+    pooleds.wait(3)
+    gbars.wait(3)
+    for gather in (img, gbars, texts, pooleds):
+        gather.wait_sent()
+    mp_copy.wait_send()
+    t_copy.wait_send()
+
+
+def whole(tokens, share, images, pair_group, own_group, w_up, w_down, total):
+    count, width = tokens.shape
+    captions = images.shape[0]
+    hidden = w_up.shape[0]
+    slab = slab_width(hidden)
+    padded = 2 * SLABS * slab
+    rows = width // 8
     own_rows = rows // 2
     bf16, f32 = jnp.bfloat16, jnp.float32
     vmem = pl.BlockSpec(memory_space=pltpu.VMEM)
+    hbm = pl.BlockSpec(memory_space=pl.ANY)
     dma = pltpu.SemaphoreType.DMA
-    flops = 4 * features * tokens * slope.shape[1] // 2
+    shape = jax.ShapeDtypeStruct
     return pl.pallas_call(
-        sum_over_chips_kernel,
-        out_shape=jax.ShapeDtypeStruct((own_rows, slope.shape[1]), f32),
-        in_specs=[vmem] * 5,
-        out_specs=vmem,
+        functools.partial(whole_kernel, total),
+        out_shape=(
+            shape((captions, LANES), f32),
+            shape((captions, width), f32),
+            shape((own_rows, padded), f32),
+            shape((total, width), bf16),
+            shape((total, hidden), bf16),
+        ),
+        in_specs=[vmem] * 7 + [hbm] * 2,
+        out_specs=(vmem,) * 5,
         scratch_shapes=[
-            pltpu.VMEM(slope.shape, bf16),
-            pltpu.VMEM((SLABS, tokens, width), bf16),
-            pltpu.VMEM((4, SLABS, rows, width), f32),
-            pltpu.VMEM((4 * SLABS, rows, width), bf16),
-            pltpu.VMEM((4 * SLABS, rows, width), bf16),
-            pltpu.VMEM((2 * SLABS, rows, width), bf16),
-            pltpu.VMEM((2 * SLABS, rows, width), bf16),
-            pltpu.VMEM((SLABS, rows, width), bf16),
-            pltpu.VMEM((SLABS, rows, width), bf16),
-            pltpu.VMEM((SLABS, own_rows, width), f32),
-            pltpu.VMEM((SLABS, own_rows, width), f32),
+            pltpu.VMEM((total, width), bf16),
+            pltpu.VMEM((captions, padded), f32),
+            pltpu.VMEM((count, padded), f32),
+            pltpu.VMEM((width, count), bf16),
+            pltpu.VMEM((width, count), bf16),
+            pltpu.VMEM(w_up.shape, bf16),
+            pltpu.VMEM(w_down.shape, bf16),
+            pltpu.VMEM((count, width), bf16),
+            pltpu.VMEM((count // 2, slab), f32),
+            pltpu.VMEM((count // 2, slab), f32),
+            pltpu.VMEM((captions, padded), f32),
+            pltpu.VMEM((captions, width), f32),
+            pltpu.VMEM((total, width), bf16),
+            pltpu.VMEM((captions, width), f32),
+            pltpu.VMEM((captions, width), f32),
+            pltpu.VMEM((count, padded), bf16),
+            pltpu.VMEM((SLABS, count, slab), bf16),
+            pltpu.VMEM((4, SLABS, rows, slab), f32),
+            pltpu.VMEM((4 * SLABS, rows, slab), bf16),
+            pltpu.VMEM((4 * SLABS, rows, slab), bf16),
+            pltpu.VMEM((2 * SLABS, rows, slab), bf16),
+            pltpu.VMEM((2 * SLABS, rows, slab), bf16),
+            pltpu.VMEM((SLABS, rows, slab), bf16),
+            pltpu.VMEM((SLABS, rows, slab), bf16),
+            pltpu.VMEM((SLABS, own_rows, slab), f32),
+            pltpu.VMEM((SLABS, own_rows, slab), f32),
+            dma((2,)),
+            dma((2, 15)),
+            dma((2, 1)),
+            dma((2, 1)),
+            dma((2, 15)),
+            dma((2, 15)),
+            dma((2, 15)),
             dma((2, SLABS)),
             dma((2, 4 * SLABS)),
             dma((2, 2 * SLABS)),
@@ -509,12 +501,23 @@
             dma((2, SLABS)),
         ],
         cost_estimate=pl.CostEstimate(
-            flops=flops, bytes_accessed=4 * features * slope.shape[1], transcendentals=0
+            flops=4 * count * width * hidden, bytes_accessed=4 * width * hidden,
+            transcendentals=count * hidden,
         ),
         compiler_params=pltpu.CompilerParams(
-            collective_id=0, has_side_effects=True, vmem_limit_bytes=56 * 1024 * 1024
+            collective_id=0, has_side_effects=True, vmem_limit_bytes=60 * 1024 * 1024
         ),
-    )(own_t, other_t, hidden_grad, share, slope)
+    )(
+        tokens,
+        share,
+        images,
+        pair_group.reshape(1, total),
+        own_group.reshape(captions, 1),
+        pair_group.reshape(total, 1),
+        own_group.reshape(1, captions),
+        w_up,
+        w_down,
+    )
 
 
 def on_device(tokens, lengths, images, pair_group, w_up, w_down):
@@ -536,10 +539,11 @@
     by_chips = devices == 16 and lax.axis_size("mp") == 2 and captions == 16
     if by_chips:
         share = jnp.broadcast_to(share.reshape(captions * seq_len, 1), (captions * seq_len, LANES))
-        gbar, text_half, pooled_half, loss, hidden_grad, slope, own_t, other_t = forward(
+        loss, image_grad, up_grad, all_pooled, all_gbar = whole(
             tokens, share, images, pair_group, own_group, w_up.T, w_down.T, total
         )
         caption_loss = loss[:, 0]
+        up_grad = up_grad[:, :hidden]
     else:
         all_images = lax.all_gather(image_half, "dp", axis=0, tiled=True)
         tok_float = tokens.astype(jnp.float32)
@@ -563,17 +567,6 @@
             loss_slope(signs, signed), all_images, preferred_element_type=jnp.float32
         )
         pooled_half = through_unit(text_back, unit_text, text_scale).astype(jnp.bfloat16)
-
-    gathered = lax.all_gather(
-        jnp.concatenate([text_half, pooled_half, gbar], 1), "dp", axis=0, tiled=True
-    )
-    all_texts = gathered[:, :width]
-    all_pooled = gathered[:, width : 2 * width]
-    all_gbar = gathered[:, 2 * width :]
-
-    if by_chips:
-        up_grad = sum_over_chips(own_t, other_t, hidden_grad, share, slope)[:, :hidden]
-    else:
         hidden_grad = jnp.dot(pooled_half, w_down, preferred_element_type=jnp.float32)
         pre_grad = (
             share[:, :, None] * hidden_grad[:, None, :] * slope.reshape(captions, seq_len, hidden)
@@ -587,15 +580,23 @@
             scatter_dimension=0,
             tiled=True,
         )
-
-    signs, signed = signed_logits(
-        all_texts, pair_group[:, None], image_half, own_group[None, :]
-    )
-    image_back = lax.dot_general(
-        loss_slope(signs, signed), all_texts, (((0,), (0,)), ((), ())),
-        preferred_element_type=jnp.float32,
-    )
-    image_grad = through_unit(image_back, unit_image, image_scale)
+        gathered = lax.all_gather(
+            jnp.concatenate([text_half, pooled_half, gbar], 1), "dp", axis=0, tiled=True
+        )
+        all_texts = gathered[:, :width]
+        all_pooled = gathered[:, width : 2 * width]
+        all_gbar = gathered[:, 2 * width :]
+        unit_image, image_scale = unit_rows(images.astype(jnp.float32))
+        image_half = unit_image.astype(jnp.bfloat16)
+        signs, signed = signed_logits(
+            all_texts, pair_group[:, None], image_half, own_group[None, :]
+        )
+        image_back = lax.dot_general(
+            loss_slope(signs, signed), all_texts, (((0,), (0,)), ((), ())),
+            preferred_element_type=jnp.float32,
+        )
+        image_grad = through_unit(image_back, unit_image, image_scale)
+
     own_pooled = lax.dynamic_slice_in_dim(all_pooled, own_index * own_rows, own_rows, 1)
     down_grad = lax.dot_general(
         own_pooled, all_gbar, (((0,), (0,)), ((), ())), preferred_element_type=jnp.float32

time: 117 us -> 88.8 us (0.76)
  Pallas kernels: 90.4 us -> 76.1 us
  between operations: 14.1 us -> 0.66 us
  other arithmetic: 3.98 us -> 1.57 us
  local copies, waits for them, and re-layouts: 5.18 us -> 7.38 us
    pallas_call x2 -> x1, Pallas kernels: 90.4 us -> 76.1 us  [whole(): pl.pallas_call(functools.partial(whole_kernel, total), out_shape=(shape((...]
    dot_general x1 -> x0, matrix products: 2.11 us -> none  [on_device(): lax.dot_general(loss_slope(signs, signed), all_texts, (((0,), (0,)), ((),...]
    reshape x2 -> x3, local copies, waits for them, and re-layouts: 1.44 us -> 3.42 us  [the longest x1 1.47 us: whole(): pair_group.reshape(total, 1)]
    concatenate x1 -> x0, other arithmetic: 1.56 us -> none  [on_device(): jnp.concatenate([text_half, pooled_half, gbar], 1)]
    dot_general x1, matrix products: 1.25 us -> 2.6 us  [on_device(): lax.dot_general(own_pooled, all_gbar, (((0,), (0,)), ((), ())), preferred...]
  transfers between devices with their start and end apart: 1 -> 0, of which waited for: 0 -> 0; matrix products, arithmetic and copies ran while one was open for 2% -> 0% of each run, Pallas kernels for 48% -> 0%
where the time goes in v5:
time: 88.8 us; the launch traced here: 88.3 us
  Pallas kernels  76.1 us (86%)
  local copies, waits for them, and re-layouts  7.38 us (8%)
  matrix products  2.6 us (3%)
  other arithmetic  1.57 us (2%)
    pallas_call x1, Pallas kernels, whole(): pl.pallas_call(functools.partial(whole_kernel, total), out_shape=(shape((...  76.1 us
    dot_general x1, matrix products, on_device(): lax.dot_general(own_pooled, all_gbar, (((0,), (0,)), ((), ())), preferred...  2.6 us

profile of v5, /device:TPU:0, one launch (start us, length us, event | category | flops | bytes accessed | tf_op | source)
XLA Modules:
  0.0 88.3 jit_solution(16388174142126171897)
XLA Ops:
  0.6 0.8 convert_reduce_fusion
  1.5 1.3 %dynamic-slice_bitcast_fusion = (s32[1,16]{1,0:T(1,128)}, s32[16,1]{0,1:T(1,128)S(1)}) fusion(s32[256]{0:T(256)} %param.9, s32[]{:T(128)S(6)} %select_n.6), kind=kLoop, calls=%fused_computation.7 | loop fusion | bytes 196 | tf_op jit(solution)/shard_map/reshape | solution.py:517
  2.7 0.7 convert_divide_fusion
  3.5 0.1 div.17
  3.5 0.7 copy.13.own_group_ref
  4.2 1.5 %copy.14.group_col_ref = s32[256,1]{1,0:T(8,128)} copy(s32[256,1]{0,1:T(1,128)} %bitcast.9) | data formatting | bytes 2048 | tf_op jit(solution)/shard_map/reshape | solution.py:516
  5.7 1.0 %broadcast_in_dim.2.share_ref = f32[1024,128]{1,0:T(8,128)} broadcast(f32[1024]{0:T(1024)S(1)} %div.17), dimensions={0} | broadcast | bytes 528384 | tf_op jit(solution)/shard_map/broadcast_in_dim | solution.py:541
  6.7 76.1 %shard_map.93 = (f32[16,128]{1,0:T(8,128)}, f32[16,1152]{1,0:T(8,128)}, f32[72,2304]{1,0:T(8,128)}, bf16[256,1152]{1,0:T(8,128)(2,1)}, bf16[256,2152]{1,0:T(8,128)(2,1)}) custom-call(bf16[1024,1152]{1,0:T(8,128)(2,1)} %tok_ref.1, f32[1024,128]{1,0:T(8,128)} %broadcast_in_dim.2.share_ref, bf16[16,1152]{1,0:T(8,128)(2,1)} %img_ref.1, s32[1,256]{1,0:T(1,128)} %bitcast.10, ...), custom_call_target="tpu_custom_call" | custom-call | flops 10154409984 | bytes 9916416 | tf_op jit(solution)/shard_map/pallas_call | solution.py:452
  82.8 0.0 copy-start
  82.8 1.4 %slice_reduce_fusion = f32[16]{0:T(128)} fusion(f32[16,128]{1,0:T(8,128)} %get-tuple-element.9), kind=kLoop, calls=%fused_computation.4 | loop fusion | bytes 128 | tf_op jit(solution)/shard_map/slice | solution.py:545
  84.2 0.0 copy-start.1
  84.2 2.6 %fusion = f32[72,2152]{1,0:T(8,128)} fusion(bf16[256,2152]{1,0:T(8,128)(2,1)} %get-tuple-element.13, bf16[256,1152]{1,0:T(8,128)(2,1)} %get-tuple-element.12, s32[]{:T(128)S(6)} %select_n.7), kind=kOutput, calls=%fused_computation | convolution fusion | flops 79331328 | bytes 1799428 | tf_op jit(solution)/shard_map/dot_general | solution.py:601
  86.8 0.0 copy-done
  86.8 0.9 slice.7
  87.7 0.0 copy-done.1
  87.7 0.6 copy.16
Async XLA Ops:
  82.8 4.0 %copy-start = (f32[72,2304]{1,0:T(8,128)S(1)}, f32[72,2304]{1,0:T(8,128)}, u32[]{:S(2)}) copy-start(f32[72,2304]{1,0:T(8,128)} %get-tuple-element.11) | copy-start | bytes 1990660
  84.2 3.5 %copy-start.1 = (f32[16,1152]{1,0:T(8,128)S(1)}, f32[16,1152]{1,0:T(8,128)}, u32[]{:S(2)}) copy-start(f32[16,1152]{1,0:T(8,128)} %get-tuple-element.21) | copy-start | bytes 221188

commit v6 on v5

--- a/solution.py
+++ b/solution.py
@@ -102,10 +102,8 @@
 
 
 def whole_kernel(
-    total, tok_ref, share_ref, img_ref, group_ref, own_group_ref, group_col_ref, own_row_ref,
-    up_hbm, down_hbm,
-    loss_ref, img_grad_ref, out_ref, all_pooled, all_gbar,
-    all_text, hidden_ref, slope_ref, own_t, other_t,
+    total, tok_ref, len_ref, img_ref, group_ref, up_hbm, down_hbm, loss_ref, img_grad_ref, out_ref, down_ref, pooled_t, all_pooled,
+    all_gbar, share_ref, all_text, hidden_ref, slope_ref, own_t, other_t,
     w_up, w_down, normed, pre_a, pre_b, gmean, tmean, images, mine, theirs,
     grad_ref, grad_other, keep, x_out, x_in, near_out, near_in, far_out, far_in, swap_out, swap_in,
     local_sems, img_sems, mp_sems, t_sems, gbar_sems, text_sems, pooled_sems,
@@ -120,12 +118,34 @@
     tile = tokens // 2
     tile_captions = captions // 2
     last = hidden // width * width
+    rows = keep.shape[2]
     f32, bf16 = jnp.float32, jnp.bfloat16
 
     up_copy = pltpu.make_async_copy(up_hbm, w_up, local_sems.at[0])
     down_copy = pltpu.make_async_copy(down_hbm, w_down, local_sems.at[1])
     up_copy.start()
     down_copy.start()
+
+    def iota(shape, dim):
+        return lax.broadcasted_iota(jnp.int32, shape, dim)
+
+    def picked(chosen, values, dim):
+        return jnp.sum(jnp.where(chosen, values, 0.0), dim, keepdims=True)
+
+    shape = (tokens, captions)
+    token, caption = iota(shape, 0), iota(shape, 1)
+    length = picked(token // seq_len == caption, len_ref[...].astype(f32), 1)
+    position = (iota((tokens, 1), 0) % seq_len).astype(f32)
+    share_ref[...] = jnp.broadcast_to(
+        jnp.where(position < length, 1.0 / length, 0.0), (tokens, LANES)
+    )
+    groups = group_ref[...].astype(f32)
+    first = place.rank * captions
+    shape = (captions, total)
+    own_group = picked(iota(shape, 0) + first == iota(shape, 1), groups, 1)
+    group_col = picked(iota((total, total), 0) == iota((total, total), 1), groups, 1)
+    shape = (total, captions)
+    own_row = picked(iota(shape, 0) == iota(shape, 1) + first, group_col, 0)
 
     unit, unused = unit_rows(img_ref[...].astype(f32))
 
@@ -241,7 +261,12 @@
     mp_copy = remote(mine, theirs, mp_sems, 0, place.mp_peer())
     mp_copy.start()
     for turn in range(2):
-        own_t[:, turn * tile : (turn + 1) * tile] = normed[turn * tile : (turn + 1) * tile, :].T
+        turned = normed[turn * tile : (turn + 1) * tile, :].T
+        for owner in range(8):
+            to = (owner % 2 * 4 + owner // 2) * rows
+            own_t[to : to + rows, turn * tile : (turn + 1) * tile] = turned[
+                owner * rows : (owner + 1) * rows
+            ]
     t_copy = remote(own_t, other_t, t_sems, 0, place.peer(*core))
     t_copy.start()
     gbars.wait(0)
@@ -253,9 +278,12 @@
     text_half = unit_text.astype(bf16)
     all_text[block_of(place.rank), :] = text_half
     texts.start(0)
-    signs, signed = signed_logits(text_half, own_group_ref[...], images[...], group_ref[...])
+    signs, signed = signed_logits(text_half, own_group, images[...], groups)
     loss = jnp.sum(jnp.maximum(-signed, 0.0) + jnp.log1p(jnp.exp(-jnp.abs(signed))), 1, keepdims=True)
-    loss_ref[...] = jnp.broadcast_to(loss / total, loss_ref.shape)
+    loss_ref[...] = jnp.sum(
+        jnp.where(iota((captions, captions), 0) == iota((captions, captions), 1), loss / total, 0.0),
+        0, keepdims=True,
+    )
     text_back = jnp.dot(loss_slope(signs, signed), images[...], preferred_element_type=f32)
     pooled_half = through_unit(text_back, unit_text, text_scale).astype(bf16)
     all_pooled[block_of(place.rank), :] = pooled_half
@@ -272,7 +300,6 @@
     core_peer, x_peer = place.peer(0, 0, 0, 1), place.peer(0, 0, 1, 0)
     near_peer, far_peer = place.peer(0, 1, 0, 0), place.peer(1, 0, 0, 0)
     half = SLABS * width
-    rows = keep.shape[2]
     own_rows = rows // 2
     copy = remote
 
@@ -326,90 +353,87 @@
     pooleds.start(2)
     t_copy.wait_recv()
 
-    def block(d0, d1, x_at, slab):
-        z_at = z + d0 * (1 - 2 * low) + d1 * (2 - 4 * high)
-        at = pl.ds(pl.multiple_of((z_at * 2 + x_at) * rows, 16), rows)
+    def z_of(turn):
+        return z + (1 - turn % 2) * (1 - 2 * low) + (1 - turn // 2) * (2 - 4 * high)
+
+    def at_x(turn, slab):
+        return z_of(turn) * SLABS + slab
+
+    def blocks(x_at, slab):
+        at = pl.ds(pl.multiple_of(x_at * (4 * rows), 16), 4 * rows)
         return jnp.dot(
-            own_t[at, :], grad_ref[:, columns(core, slab)], preferred_element_type=jnp.float32
-        ) + jnp.dot(other_t[at, :], grad_other[slab], preferred_element_type=jnp.float32)
-
-    for slab in range(SLABS):
+            own_t[at, :], grad_ref[:, columns(core, slab)], preferred_element_type=f32
+        ) + jnp.dot(other_t[at, :], grad_other[slab], preferred_element_type=f32)
+
+    @pl.loop(0, SLABS)
+    def _(slab):
         grad_copy(slab).wait_recv()
-
-        @pl.loop(0, 1)
-        def _(unused, slab=slab):
-            x_out[slab] = block(1, 1, 1 - x, slab).astype(jnp.bfloat16)
-            x_copy(slab).start()
-
-    @pl.loop(SLABS, 4 * SLABS)
-    def _(step):
-        turn, slab = step // SLABS, step % SLABS
-        x_out[step] = block(1 - turn % 2, 1 - turn // 2, 1 - x, slab).astype(jnp.bfloat16)
-        x_copy(step).start()
-
-    @pl.loop(0, 4 * SLABS)
-    def _(step):
-        turn, slab = step // SLABS, step % SLABS
-        keep[step // SLABS, step % SLABS] = block(1 - turn % 2, 1 - turn // 2, x, slab)
+        sums = blocks(1 - x, slab)
+        for z_at in range(4):
+            x_out[z_at * SLABS + slab] = sums[z_at * rows : (z_at + 1) * rows].astype(bf16)
+        for turn in (0, 2, 1, 3):
+            x_copy(at_x(turn, slab)).start()
 
     gbars.wait(2)
     gbars.start(3)
-
-    @pl.loop(0, SLABS)
-    def _(slab):
-        x_copy(slab).wait_recv()
-        near_out[slab] = (keep[0, slab] + x_in[slab].astype(jnp.float32)).astype(jnp.bfloat16)
-        near_copy(slab).start()
-
-    @pl.loop(0, SLABS)
-    def _(slab):
-        x_copy(SLABS + slab).wait_recv()
-        near_copy(slab).wait_recv()
-        far_out[slab] = (
-            keep[1, slab]
-            + x_in[SLABS + slab].astype(jnp.float32)
-            + near_in[slab].astype(jnp.float32)
-        ).astype(jnp.bfloat16)
-        far_copy(slab).start()
-
-    @pl.loop(0, SLABS)
-    def _(slab):
-        x_copy(2 * SLABS + slab).wait_recv()
-        near_out[SLABS + slab] = (
-            keep[2, slab] + x_in[2 * SLABS + slab].astype(jnp.float32)
-        ).astype(jnp.bfloat16)
-        near_copy(SLABS + slab).start()
-
     texts.wait(2)
     texts.start(3)
     pooleds.wait(2)
     pooleds.start(3)
+
+    @pl.loop(0, SLABS)
+    def _(slab):
+        sums = blocks(x, slab)
+        for z_at in range(4):
+            keep[z_at, slab] = sums[z_at * rows : (z_at + 1) * rows]
+
+    def from_x(turn, slab):
+        x_copy(at_x(turn, slab)).wait_recv()
+        return keep[z_of(turn), slab] + x_in[at_x(turn, slab)].astype(f32)
+
+    def forward_sums(slab):
+        near_out[slab] = from_x(0, slab).astype(bf16)
+        near_copy(slab).start()
+        near_out[SLABS + slab] = from_x(2, slab).astype(bf16)
+        near_copy(SLABS + slab).start()
+        partial = from_x(1, slab)
+        near_copy(slab).wait_recv()
+        far_out[slab] = (partial + near_in[slab].astype(f32)).astype(bf16)
+        far_copy(slab).start()
+
+    def finish(slab):
+        partial = from_x(3, slab)
+        near_copy(SLABS + slab).wait_recv()
+        far_copy(slab).wait_recv()
+        keep[z, slab] = (
+            partial + near_in[SLABS + slab].astype(f32) + far_in[slab].astype(f32)
+        )
+        peers = pl.ds(pl.multiple_of((1 - core) * own_rows, 8), own_rows)
+        ours = pl.ds(pl.multiple_of(core * own_rows, 8), own_rows)
+        swap_out[slab] = keep[z, slab, peers, :]
+        swap_copy(slab).start()
+        out_ref[:, columns(core, slab)] = keep[z, slab, ours, :]
+
+    forward_sums(0)
+
     unit_image, image_scale = unit_rows(img_ref[...].astype(f32))
     texts.wait(3)
-    signs, signed = signed_logits(
-        all_text[...], group_col_ref[...], unit_image.astype(bf16), own_row_ref[...]
-    )
+    signs, signed = signed_logits(all_text[...], group_col, unit_image.astype(bf16), own_row)
     image_back = lax.dot_general(
         loss_slope(signs, signed), all_text[...], (((0,), (0,)), ((), ())),
         preferred_element_type=f32,
     )
     img_grad_ref[...] = through_unit(image_back, unit_image, image_scale)
-
-    for slab in range(SLABS):
-        x_copy(3 * SLABS + slab).wait_recv()
-        near_copy(SLABS + slab).wait_recv()
-        far_copy(slab).wait_recv()
-        keep[3, slab] = (
-            keep[3, slab]
-            + x_in[3 * SLABS + slab].astype(jnp.float32)
-            + near_in[SLABS + slab].astype(jnp.float32)
-            + far_in[slab].astype(jnp.float32)
-        )
-        theirs = pl.ds(pl.multiple_of((1 - core) * own_rows, 8), own_rows)
-        mine = pl.ds(pl.multiple_of(core * own_rows, 8), own_rows)
-        swap_out[slab] = keep[3, slab, theirs, :]
-        swap_copy(slab).start()
-        out_ref[:, columns(core, slab)] = keep[3, slab, mine, :]
+    pooleds.wait(3)
+    gbars.wait(3)
+    pooled_t[...] = all_pooled[...].astype(f32).T
+    own_pooled = pooled_t[pl.ds(pl.multiple_of(place.rank * own_rows, 8), own_rows), :]
+    down_ref[...] = jnp.dot(own_pooled.astype(bf16), all_gbar[...], preferred_element_type=f32)
+
+    for slab in range(1, SLABS):
+        forward_sums(slab)
+        finish(slab - 1)
+    finish(SLABS - 1)
 
     for slab in range(SLABS):
         swap_copy(slab).wait_recv()
@@ -428,15 +452,13 @@
     def _(step):
         near_copy(step).wait_send()
 
-    pooleds.wait(3)
-    gbars.wait(3)
     for gather in (img, gbars, texts, pooleds):
         gather.wait_sent()
     mp_copy.wait_send()
     t_copy.wait_send()
 
 
-def whole(tokens, share, images, pair_group, own_group, w_up, w_down, total):
+def whole(tokens, lengths, images, pair_group, w_up, w_down, total):
     count, width = tokens.shape
     captions = images.shape[0]
     hidden = w_up.shape[0]
@@ -452,15 +474,18 @@
     return pl.pallas_call(
         functools.partial(whole_kernel, total),
         out_shape=(
-            shape((captions, LANES), f32),
+            shape((1, captions), f32),
             shape((captions, width), f32),
             shape((own_rows, padded), f32),
-            shape((total, width), bf16),
-            shape((total, hidden), bf16),
+            shape((own_rows, hidden), f32),
         ),
-        in_specs=[vmem] * 7 + [hbm] * 2,
-        out_specs=(vmem,) * 5,
+        in_specs=[vmem] * 4 + [hbm] * 2,
+        out_specs=(vmem,) * 4,
         scratch_shapes=[
+            pltpu.VMEM((width, total), f32),
+            pltpu.VMEM((total, width), bf16),
+            pltpu.VMEM((total, hidden), bf16),
+            pltpu.VMEM((count, LANES), f32),
             pltpu.VMEM((total, width), bf16),
             pltpu.VMEM((captions, padded), f32),
             pltpu.VMEM((count, padded), f32),
@@ -509,12 +534,9 @@
         ),
     )(
         tokens,
-        share,
+        lengths.reshape(1, captions),
         images,
         pair_group.reshape(1, total),
-        own_group.reshape(captions, 1),
-        pair_group.reshape(total, 1),
-        own_group.reshape(1, captions),
         w_up,
         w_down,
     )
@@ -538,11 +560,10 @@
 
     by_chips = devices == 16 and lax.axis_size("mp") == 2 and captions == 16
     if by_chips:
-        share = jnp.broadcast_to(share.reshape(captions * seq_len, 1), (captions * seq_len, LANES))
-        loss, image_grad, up_grad, all_pooled, all_gbar = whole(
-            tokens, share, images, pair_group, own_group, w_up.T, w_down.T, total
-        )
-        caption_loss = loss[:, 0]
+        loss, image_grad, up_grad, down_grad = whole(
+            tokens, lengths, images, pair_group, w_up.T, w_down.T, total
+        )
+        caption_loss = loss.reshape(captions)
         up_grad = up_grad[:, :hidden]
     else:
         all_images = lax.all_gather(image_half, "dp", axis=0, tiled=True)
@@ -596,11 +617,10 @@
             preferred_element_type=jnp.float32,
         )
         image_grad = through_unit(image_back, unit_image, image_scale)
-
-    own_pooled = lax.dynamic_slice_in_dim(all_pooled, own_index * own_rows, own_rows, 1)
-    down_grad = lax.dot_general(
-        own_pooled, all_gbar, (((0,), (0,)), ((), ())), preferred_element_type=jnp.float32
-    )
+        own_pooled = lax.dynamic_slice_in_dim(all_pooled, own_index * own_rows, own_rows, 1)
+        down_grad = lax.dot_general(
+            own_pooled, all_gbar, (((0,), (0,)), ((), ())), preferred_element_type=jnp.float32
+        )
     return (caption_loss, image_grad, up_grad, down_grad)
 
 

time: 88.8 us -> 87.3 us (0.983)
  Pallas kernels: 76.1 us -> 79.9 us
  matrix products: 2.6 us -> 0 us
  other arithmetic: 1.57 us -> 0 us
  local copies, waits for them, and re-layouts: 7.38 us -> 6.49 us
    unnamed x5 -> x3, local copies, waits for them, and re-layouts: 0.64 us -> 4.55 us
    pallas_call x1, Pallas kernels: 76.1 us -> 79.9 us  [whole(): pl.pallas_call(functools.partial(whole_kernel, total), out_shape=(shape((...]
    reshape x3 -> x0, local copies, waits for them, and re-layouts: 3.42 us -> none  [the longest x1 1.47 us: whole(): pair_group.reshape(total, 1)]
    dot_general x1 -> x0, matrix products: 2.6 us -> none  [on_device(): lax.dot_general(own_pooled, all_gbar, (((0,), (0,)), ((), ())), preferred...]
    slice x1 -> x0, local copies, waits for them, and re-layouts: 1.39 us -> none  [on_device(): caption_loss = loss[:, 0]]
    slice x1, local copies, waits for them, and re-layouts: 0.87 us -> 1.95 us  [on_device(): up_grad = up_grad[:, :hidden]]
    broadcast_in_dim x1 -> x0, local copies, waits for them, and re-layouts: 0.99 us -> none  [on_device(): jnp.broadcast_to(share.reshape(captions * seq_len, 1), (captions * seq_le...]
where the time goes in v6:
time: 87.3 us; the launch traced here: 87 us
  Pallas kernels  79.9 us (92%)
  local copies, waits for them, and re-layouts  6.49 us (7%)
    pallas_call x1, Pallas kernels, whole(): pl.pallas_call(functools.partial(whole_kernel, total), out_shape=(shape((...  79.9 us
    unnamed x3, local copies, waits for them, and re-layouts  4.55 us
    slice x1, local copies, waits for them, and re-layouts, on_device(): up_grad = up_grad[:, :hidden]  1.95 us

profile of v6, /device:TPU:0, one launch (start us, length us, event | category | flops | bytes accessed | tf_op | source)
XLA Modules:
  0.0 87.0 jit_solution(11496387908900646085)
XLA Ops:
  0.6 79.9 %shard_map.93 = (f32[1,16]{1,0:T(1,128)}, f32[16,1152]{1,0:T(8,128)}, f32[72,2304]{1,0:T(8,128)}, f32[72,2152]{1,0:T(8,128)}) custom-call(bf16[1024,1152]{1,0:T(8,128)(2,1)} %tok_ref.1, s32[1,16]{1,0:T(1,128)} %bitcast.8, bf16[16,1152]{1,0:T(8,128)(2,1)} %img_ref.1, s32[1,256]{1,0:T(1,128)} %bitcast.7, bf16[2152,1152]{1,0:T(8,128)(2,1)} %bitcast.5, ...), custom_call_target="tpu_custom_call" | custom-call | flops 10154409984 | bytes 9916416 | tf_op jit(solution)/shard_map/pallas_call | solution.py:474
  80.5 1.9 %slice.3 = f32[72,2152]{1,0:T(8,128)} slice(f32[72,2304]{1,0:T(8,128)} %get-tuple-element.10), slice={[0:72], [0:2152]} | slice | bytes 1239552 | tf_op jit(solution)/shard_map/slice | solution.py:567
  82.4 1.1 %copy.13 = f32[16]{0:T(128)} copy(f32[16]{0:T(128)} %bitcast.9) | data formatting | bytes 128
  83.5 1.5 %copy.14 = f32[16,1152]{1,0:T(8,128)} copy(f32[16,1152]{1,0:T(8,128)} %get-tuple-element.17) | data formatting | bytes 147456
  85.0 1.9 %copy.15 = f32[72,2152]{1,0:T(8,128)} copy(f32[72,2152]{1,0:T(8,128)} %get-tuple-element.19) | data formatting | bytes 1239552

commit v7 on v6

--- a/solution.py
+++ b/solution.py
@@ -160,16 +160,18 @@
     stages = (far, near, across, core)
 
     class Gather:
-        def __init__(self, ref, sems):
-            self.ref, self.sems = ref, sems
+        def __init__(self, ref, sems, order):
+            self.ref, self.sems, self.order = ref, sems, order
 
         def copies(self, stage):
             result = []
             for held in range(1 << stage):
-                flips = [(held >> bit) & 1 if bit < stage else 0 for bit in range(4)]
+                flips = [0] * 4
+                for bit in range(stage):
+                    flips[self.order[bit]] = (held >> bit) & 1
                 part = self.ref.at[block_of(place.toward(*flips)), :]
                 index = (1 << stage) - 1 + held
-                result.append(remote(part, part, self.sems, index, place.peer(*stages[stage])))
+                result.append(remote(part, part, self.sems, index, place.peer(*stages[self.order[stage]])))
             return result
 
         def start(self, stage):
@@ -185,8 +187,9 @@
                 for c in self.copies(stage):
                     c.wait_send()
 
-    img, gbars = Gather(images, img_sems), Gather(all_gbar, gbar_sems)
-    texts, pooleds = Gather(all_text, text_sems), Gather(all_pooled, pooled_sems)
+    img, gbars = Gather(images, img_sems, (0, 1, 2, 3)), Gather(all_gbar, gbar_sems, (2, 0, 1, 3))
+    texts = Gather(all_text, text_sems, (0, 2, 1, 3))
+    pooleds = Gather(all_pooled, pooled_sems, (0, 2, 1, 3))
 
     img.start(0)
 
@@ -288,8 +291,6 @@
     pooled_half = through_unit(text_back, unit_text, text_scale).astype(bf16)
     all_pooled[block_of(place.rank), :] = pooled_half
     pooleds.start(0)
-    gbars.wait(1)
-    gbars.start(2)
     hidden_ref[:, last:] = jnp.zeros((captions, hidden_ref.shape[1] - last), f32)
     hidden_ref[:, :hidden] = lax.dot_general(
         pooled_half, w_down[...], (((1,), (1,)), ((), ())), preferred_element_type=f32
@@ -342,6 +343,8 @@
     texts.start(1)
     pooleds.wait(0)
     pooleds.start(1)
+    gbars.wait(1)
+    gbars.start(2)
 
     @pl.loop(0, SLABS)
     def _(slab):

time: 87.3 us -> 86.8 us (level)
  no operation moved by 1% of the time
where the time goes in v7:
time: 86.8 us; the launch traced here: 86.5 us
  Pallas kernels  79.4 us (91%)
  local copies, waits for them, and re-layouts  6.49 us (7%)
    pallas_call x1, Pallas kernels, whole(): pl.pallas_call(functools.partial(whole_kernel, total), out_shape=(shape((...  79.4 us
    unnamed x3, local copies, waits for them, and re-layouts  4.55 us
    slice x1, local copies, waits for them, and re-layouts, on_device(): up_grad = up_grad[:, :hidden]  1.95 us

profile of v7, /device:TPU:0, one launch (start us, length us, event | category | flops | bytes accessed | tf_op | source)
XLA Modules:
  0.0 86.5 jit_solution(9195502805084880286)
XLA Ops:
  0.6 79.4 %shard_map.93 = (f32[1,16]{1,0:T(1,128)}, f32[16,1152]{1,0:T(8,128)}, f32[72,2304]{1,0:T(8,128)}, f32[72,2152]{1,0:T(8,128)}) custom-call(bf16[1024,1152]{1,0:T(8,128)(2,1)} %tok_ref.1, s32[1,16]{1,0:T(1,128)} %bitcast.8, bf16[16,1152]{1,0:T(8,128)(2,1)} %img_ref.1, s32[1,256]{1,0:T(1,128)} %bitcast.7, bf16[2152,1152]{1,0:T(8,128)(2,1)} %bitcast.5, ...), custom_call_target="tpu_custom_call" | custom-call | flops 10154409984 | bytes 9916416 | tf_op jit(solution)/shard_map/pallas_call | solution.py:477
  80.0 1.9 %slice.3 = f32[72,2152]{1,0:T(8,128)} slice(f32[72,2304]{1,0:T(8,128)} %get-tuple-element.10), slice={[0:72], [0:2152]} | slice | bytes 1239552 | tf_op jit(solution)/shard_map/slice | solution.py:570
  81.9 1.1 %copy.13 = f32[16]{0:T(128)} copy(f32[16]{0:T(128)} %bitcast.9) | data formatting | bytes 128
  83.0 1.5 %copy.14 = f32[16,1152]{1,0:T(8,128)} copy(f32[16,1152]{1,0:T(8,128)} %get-tuple-element.17) | data formatting | bytes 147456
  84.5 1.9 %copy.15 = f32[72,2152]{1,0:T(8,128)} copy(f32[72,2152]{1,0:T(8,128)} %get-tuple-element.19) | data formatting | bytes 1239552
